TPU v7x, 256 devices: a whole 4x4x8 slice. The times are simulated.
256 devices in a mesh: tm: 32 (over x, z_lo, core), space: 8 (over y, z_hi).
Axes of the slice: x: 4, y: 4, z: 8 (z_hi: 2, z_lo: 4; z = z_hi * 4 + z_lo), core: 2. Of those that a mesh axis runs over, the one named last changes fastest.
Arguments:
- initial: float32 [64, 64, 128], P('space'), may hold values from -6 to 6
- forcing: bfloat16 [128, 64, 64, 128], P('tm', 'space'), may hold values from -4 to 4
- brick_blocks: bfloat16 [64, 64, 448], P('space'), may hold values from -1 to 1
- neighbours: int32 [64, 6], P('space'), may hold values from 0 to 63, as said below
- coarse_modes: float32 [8, 64], replicated, may hold values from -0.75 to 0.75
- coarse_blocks: float32 [64, 8, 8], P('space'), may hold values from -1 to 1.2
Outputs:
- solution: float32 [128, 64, 64, 128], P('tm', 'space')
- last_defect: float32 [32, 64, 64, 128], P('tm', 'space')
Inputs may be any that keep to these rules, and one draw needn't show every extreme that they name: `neighbours`: each brick's 6 slots name distinct bricks other than itself, in a random slot order, each at most 4 positions away along the periodic brick order; every brick names the bricks directly before and after it and one brick exactly 4 away.
All inputs are finite; a program needn't handle non-finite values.
Results may differ from a plain program's by a relative error of at most 0.014.
Values may be sent and summed in bfloat16 or wider, within the bound.
A program may use at most 64 MiB of HBM per device.

v0:
```python
import functools

import jax
import jax.numpy as jnp
from jax import lax
from jax.experimental import pallas as pl
from jax.experimental.pallas import tpu as pltpu
from jax.sharding import PartitionSpec as P

BRICK = 64
ENS = 128
NB = 6
REACH = 4
Q = 8
STEPS = 4
ITERS = 2
HERE = 8
SLICES = 32
ROWS = HERE * BRICK
HALF = ROWS // 2

MESH = pl.DeviceIdType.MESH
HIGHEST = lax.Precision.HIGHEST
F32 = jnp.float32
BF16 = jnp.bfloat16


def dot(a, b):
    return jnp.dot(a, b, preferred_element_type=F32)


def dot32(a, b):
    return jnp.dot(a, b, preferred_element_type=F32, precision=HIGHEST)


def kernel(
    init_ref, forcing_ref, blocks_ref, neighbours_ref, modes_ref, coarse_ref,
    sol_ref, def_ref,
    fields, weights, home_nbr, nbr, start, state, band, diag, ext0, ext1,
    restrict, toep, strip, r_buf, in0, in1, e_buf, got0, got1, e_prev, e_here, ends, stage,
    field_sem, weight_sem, nbr_sem, start_sem, halo_send, halo_recv,
    swap_send, sc_send, sc_recv, out_send, sol_recv, def_recv,
):
    tm = lax.axis_index("tm")
    sp = lax.axis_index("space")
    c = lax.rem(tm, 2)
    zl = lax.rem(tm // 2, 4)
    x = tm // 8
    y = sp // 2
    zh = lax.rem(sp, 2)
    keeps = c == zh
    moves = c != zh
    j = x * 8 + zl * 2 + zh
    q = 2 * y + c
    partner = (tm - c + zh, sp - zh + c)
    q_low = lax.rem(q + 7, 8)
    q_high = lax.rem(q + 1, 8)
    low = (tm - c + lax.rem(q_low, 2), (q_low // 2) * 2 + zh)
    high = (tm - c + lax.rem(q_high, 2), (q_high // 2) * 2 + zh)

    def worker(slice_id):
        return (
            (slice_id // 8) * 8 + lax.rem(slice_id // 2, 4) * 2 + c,
            2 * y + lax.rem(slice_id, 2),
        )

    barrier = pltpu.get_barrier_semaphore()
    pl.semaphore_signal(barrier, inc=1, device_id=low, device_id_type=MESH)
    pl.semaphore_signal(barrier, inc=1, device_id=high, device_id_type=MESH)

    @pl.when(moves)
    def _():
        pl.semaphore_signal(barrier, inc=1, device_id=partner, device_id_type=MESH)

    @pl.loop(1, SLICES)
    def _(d):
        pl.semaphore_signal(
            barrier, inc=1, device_id=worker(lax.rem(j + d, SLICES)), device_id_type=MESH
        )

    home_nbr[...] = jnp.zeros_like(home_nbr)
    home_nbr[:, 0:NB] = neighbours_ref[...]
    pl.semaphore_wait(barrier, jnp.where(moves, SLICES + 2, SLICES + 1))

    def remote(src, dst, send, recv, device):
        return pltpu.make_async_remote_copy(
            src_ref=src, dst_ref=dst, send_sem=send, recv_sem=recv,
            device_id=device, device_id_type=MESH,
        )

    def arrived(ref, sem):
        pltpu.make_async_copy(ref, ref, sem).wait()

    @pl.when(keeps)
    def _():
        pltpu.make_async_copy(blocks_ref, weights, weight_sem).start()
        for i in range(STEPS):
            pltpu.make_async_copy(forcing_ref.at[i], fields.at[i], field_sem.at[i]).start()
        pltpu.make_async_copy(home_nbr, nbr, nbr_sem).start()

    @pl.when(moves)
    def _():
        remote(home_nbr, nbr, swap_send.at[5], nbr_sem, partner).start()
        remote(blocks_ref, weights, swap_send.at[4], weight_sem, partner).start()
        for i in range(STEPS):
            remote(
                forcing_ref.at[i], fields.at[i], swap_send.at[i], field_sem.at[i], partner
            ).start()

    @pl.when((tm == 0) & (zh == 1))
    def _():
        remote(init_ref, start, swap_send.at[6], start_sem, partner).start()

    @pl.when((tm == 0) & (zh == 0))
    def _():
        pltpu.make_async_copy(init_ref, start, start_sem).start()

    modes = modes_ref[...]
    wide = jnp.concatenate([jnp.concatenate([modes] * 4, axis=1)] * 4, axis=0)
    row = lax.broadcasted_iota(jnp.int32, (4 * Q, HALF), 0)
    col = lax.broadcasted_iota(jnp.int32, (4 * Q, HALF), 1)
    restrict[...] = jnp.where(row // Q == col // BRICK, wide, 0.0)

    own_brick = lax.rem(x, 2) * 4 + zl
    half = x // 2
    one = coarse_ref[own_brick]
    eye = (
        lax.broadcasted_iota(jnp.int32, (Q, Q), 0) == lax.broadcasted_iota(jnp.int32, (Q, Q), 1)
    ).astype(F32)
    powers = eye
    power = one
    while powers.shape[1] < SLICES * Q:
        powers = jnp.concatenate([dot32(power, powers), powers], axis=1)
        power = dot32(power, power)
    strip[:, 0 : SLICES * Q] = powers
    strip[:, SLICES * Q :] = jnp.zeros((Q, SLICES * Q), F32)
    both = strip[...]
    for i in range(SLICES):
        first = (SLICES - 1 - i) * Q
        toep[i * Q : (i + 1) * Q, :] = both[:, first : first + SLICES * Q]
    e_buf[0] = jnp.zeros((Q, ENS), F32)

    diag[...] = jnp.zeros_like(diag)
    band[...] = jnp.zeros_like(band)
    arrived(nbr, nbr_sem)
    arrived(weights, weight_sem)
    position = 8 * q + lax.broadcasted_iota(jnp.int32, (HERE, 128), 0)
    shift = lax.rem(nbr[...] - position + (REACH + 64), 64)
    for b in range(HERE):
        g, b4 = divmod(b, 4)
        rows = slice(b4 * BRICK, (b4 + 1) * BRICK)
        diag[g, rows, rows] = weights[b, :, 0:BRICK]
        offs = [weights[b, :, (k + 1) * BRICK : (k + 2) * BRICK].astype(F32) for k in range(NB)]
        where = [jnp.broadcast_to(shift[b : b + 1, k : k + 1], (BRICK, BRICK)) for k in range(NB)]
        for p in range(2 * REACH + 1):
            block = jnp.zeros((BRICK, BRICK), F32)
            for k in range(NB):
                block = jnp.where(where[k] == p, offs[k], block)
            first = (b4 + p) * BRICK
            band[g, rows, first : first + BRICK] = block.astype(BF16)

    def exchange(ext, values, slot):
        ext[HALF : 2 * HALF, :] = values(0).astype(BF16)
        down = remote(
            ext.at[pl.ds(HALF, HALF)], ext.at[pl.ds(3 * HALF, HALF)],
            halo_send.at[slot, 0], halo_recv.at[slot, 0], low,
        )
        down.start()
        ext[2 * HALF : 3 * HALF, :] = values(1).astype(BF16)
        up = remote(
            ext.at[pl.ds(2 * HALF, HALF)], ext.at[pl.ds(0, HALF)],
            halo_send.at[slot, 1], halo_recv.at[slot, 1], high,
        )
        up.start()
        near0 = dot(band[0, :, HALF:], ext[HALF : 3 * HALF, :])
        near1 = dot(band[1, :, : 2 * HALF], ext[HALF : 3 * HALF, :])
        down.wait_send()
        up.wait_send()
        down.wait_recv()
        up.wait_recv()
        return (
            near0 + dot(band[0, :, :HALF], ext[0:HALF, :]),
            near1 + dot(band[1, :, 2 * HALF :], ext[3 * HALF :, :]),
        )

    def propagate():
        values = [state[0:HALF, :], state[HALF:ROWS, :]]
        coupled = exchange(ext0, lambda g: dot(diag[g], values[g].astype(BF16)), 0)
        coupled = exchange(
            ext1, lambda g: dot(diag[g], (values[g] - coupled[g]).astype(BF16)), 1
        )
        return [dot(diag[g], (values[g] - coupled[g]).astype(BF16)) for g in range(2)]

    def halves(g):
        return slice(g * HALF, (g + 1) * HALF)

    def step(i):
        following = propagate()
        for g in range(2):
            state[halves(g), :] = following[g] + fields[i, halves(g), :].astype(F32)

    def deliver(n):
        target = sol_ref.at[n] if n < STEPS else def_ref

        @pl.when(keeps)
        def _():
            pltpu.make_async_copy(
                stage.at[n], target, sol_recv if n < STEPS else def_recv
            ).start()

        @pl.when(moves)
        def _():
            remote(
                stage.at[n], target, out_send.at[n], sol_recv if n < STEPS else def_recv, partner
            ).start()

    @pl.when(j == 0)
    def _():
        arrived(start, start_sem)
        state[...] = start[...]

    @pl.when(j != 0)
    def _():
        state[...] = jnp.zeros_like(state)

    ends[...] = jnp.zeros_like(ends)
    e_prev[...] = jnp.zeros_like(e_prev)
    e_here[...] = jnp.zeros_like(e_here)

    for it, (incoming, got) in enumerate(((in0, got0), (in1, got1))):

        @pl.loop(0, STEPS)
        def _(i):
            if it == 0:
                arrived(fields.at[i], field_sem.at[i])
            step(i)

        for g in range(2):
            defect = state[halves(g), :] - ends[halves(g), :]
            if it == ITERS - 1:
                stage[STEPS, halves(g), :] = defect.astype(BF16)
            r_buf[it, 4 * g : 4 * g + 4] = dot32(restrict[...], defect).reshape(4, Q, ENS)

        @pl.loop(0, 16)
        def _(w):
            brick = lax.rem(w, 8)
            owner_tm = ((w // 8) * 2 + brick // 4) * 8 + lax.rem(brick, 4) * 2 + c
            owner_sp = 2 * y + c
            mine = (owner_tm == tm) & (owner_sp == sp)

            @pl.when(mine)
            def _():
                incoming[j] = r_buf[it, brick]

            @pl.when(jnp.logical_not(mine))
            def _():
                remote(
                    r_buf.at[it, brick], incoming.at[j], sc_send.at[it, 0], sc_recv.at[it, 0],
                    (owner_tm, owner_sp),
                ).start()

        if it == ITERS - 1:
            deliver(STEPS)

        @pl.when(keeps)
        def _():
            arrived(incoming.at[pl.ds(0, SLICES - 1)], sc_recv.at[it, 0])
            errors = dot32(toep[...], incoming[...].reshape(SLICES * Q, ENS))
            if it:
                arrived(e_buf.at[pl.ds(0, 30)], sc_send.at[0, 1])
            e_buf[1:] = errors.reshape(SLICES, Q, ENS)

            @pl.loop(0, 16)
            def _(d):
                there = half * 16 + d

                @pl.when(there == j)
                def _():
                    got[own_brick] = e_buf[pl.ds(j, 2)]

                @pl.when(there != j)
                def _():
                    remote(
                        e_buf.at[pl.ds(there, 2)], got.at[own_brick],
                        sc_send.at[it, 1], sc_recv.at[it, 1], worker(there),
                    ).start()

            arrived(got.at[pl.ds(0, 7)], sc_recv.at[it, 1])
            arrived(incoming.at[pl.ds(0, 15)], sc_send.at[it, 0])

        @pl.when(moves)
        def _():
            arrived(got, sc_recv.at[it, 1])
            arrived(incoming.at[pl.ds(0, 16)], sc_send.at[it, 0])

        e_prev[...] += got[:, 0].reshape(HERE * Q, ENS)
        e_here[...] += got[:, 1].reshape(HERE * Q, ENS)
        prolong = restrict[...].T
        for g in range(2):
            part = slice(g * 4 * Q, (g + 1) * 4 * Q)
            ends[halves(g), :] = dot32(prolong, e_here[part, :])

        @pl.when(j == 0)
        def _():
            state[...] = start[...]

        @pl.when(j != 0)
        def _():
            for g in range(2):
                part = slice(g * 4 * Q, (g + 1) * 4 * Q)
                state[halves(g), :] = dot32(prolong, e_prev[part, :])

    stage[STEPS - 1] = ends[...].astype(BF16)
    deliver(STEPS - 1)
    for i in range(STEPS - 1):
        step(i)
        stage[i] = state[...].astype(BF16)
        deliver(i)

    @pl.when(keeps)
    def _():
        arrived(e_buf.at[pl.ds(0, 30)], sc_send.at[1, 1])

    @pl.when(moves)
    def _():
        arrived(home_nbr, swap_send.at[5])
        arrived(weights, swap_send.at[4])
        for i in range(STEPS):
            arrived(fields.at[i], swap_send.at[i])
        for n in range(STEPS + 1):
            arrived(stage.at[n], out_send.at[n])

    @pl.when((tm == 0) & (zh == 1))
    def _():
        arrived(start, swap_send.at[6])

    arrived(sol_ref, sol_recv)
    arrived(def_ref, def_recv)


def body(initial, forcing, brick_blocks, neighbours, coarse_modes, coarse_blocks):
    vmem = pl.BlockSpec(memory_space=pltpu.VMEM)
    hbm = pl.BlockSpec(memory_space=pl.ANY)
    sem = pltpu.SemaphoreType.DMA
    sol, last = pl.pallas_call(
        kernel,
        out_shape=(
            jax.ShapeDtypeStruct((STEPS, ROWS, ENS), BF16),
            jax.ShapeDtypeStruct((ROWS, ENS), BF16),
        ),
        in_specs=[hbm, hbm, hbm, vmem, vmem, vmem],
        out_specs=(hbm, hbm),
        scratch_shapes=[
            pltpu.VMEM((STEPS, ROWS, ENS), BF16),
            pltpu.VMEM((HERE, BRICK, (NB + 1) * BRICK), BF16),
            pltpu.VMEM((HERE, 128), jnp.int32),
            pltpu.VMEM((HERE, 128), jnp.int32),
            pltpu.VMEM((ROWS, ENS), F32),
            pltpu.VMEM((ROWS, ENS), F32),
            pltpu.VMEM((2, HALF, 3 * HALF), BF16),
            pltpu.VMEM((2, HALF, HALF), BF16),
            pltpu.VMEM((4 * HALF, ENS), BF16),
            pltpu.VMEM((4 * HALF, ENS), BF16),
            pltpu.VMEM((4 * Q, HALF), F32),
            pltpu.VMEM((SLICES * Q, SLICES * Q), F32),
            pltpu.VMEM((Q, 2 * SLICES * Q), F32),
            pltpu.VMEM((ITERS, HERE, Q, ENS), F32),
            pltpu.VMEM((SLICES, Q, ENS), F32),
            pltpu.VMEM((SLICES, Q, ENS), F32),
            pltpu.VMEM((SLICES + 1, Q, ENS), F32),
            pltpu.VMEM((HERE, 2, Q, ENS), F32),
            pltpu.VMEM((HERE, 2, Q, ENS), F32),
            pltpu.VMEM((HERE * Q, ENS), F32),
            pltpu.VMEM((HERE * Q, ENS), F32),
            pltpu.VMEM((ROWS, ENS), F32),
            pltpu.VMEM((STEPS + 1, ROWS, ENS), BF16),
            sem((STEPS,)),
            sem,
            sem,
            sem,
            sem((2, 2)),
            sem((2, 2)),
            sem((7,)),
            sem((ITERS, 2)),
            sem((ITERS, 2)),
            sem((STEPS + 1,)),
            sem,
            sem,
        ],
        compiler_params=pltpu.CompilerParams(
            collective_id=0, has_side_effects=True, vmem_limit_bytes=48 * 2**20
        ),
    )(
        initial.reshape(ROWS, ENS),
        forcing.reshape(STEPS, ROWS, ENS),
        brick_blocks,
        neighbours,
        coarse_modes,
        coarse_blocks,
    )
    return (
        sol.astype(F32).reshape(STEPS, HERE, BRICK, ENS),
        last.astype(F32).reshape(1, HERE, BRICK, ENS),
    )


def solution(mesh):
    placed = (
        P("space", None, None),
        P("tm", "space", None, None),
        P("space", None, None),
        P("space", None),
        P(),
        P("space", None, None),
    )
    return jax.shard_map(
        body,
        mesh=mesh,
        in_specs=placed,
        out_specs=(P("tm", "space", None, None), P("tm", "space", None, None)),
        check_vma=False,
    )
```

profile of v0, /device:TPU:7, one launch (start us, length us, event | category | flops | bytes accessed | tf_op | source)
XLA Modules:
  0.0 174.6 jit_solution(16457073968483675671)
XLA Ops:
  0.6 0.0 copy-start
  0.6 1.0 copy-done
  1.7 0.0 copy-start.1
  1.7 1.0 copy-done.1
  2.7 0.0 copy-start.2
  2.7 0.9 copy-done.2
  3.7 0.0 copy-start.3
  3.7 0.8 copy-done.3
  4.4 0.0 copy-start.4
  4.4 0.7 copy-done.4
  5.1 0.0 copy-start.5
  5.1 0.7 copy-done.5
  5.8 167.0 %shard_map.77 = (bf16[4,512,128]{2,1,0:T(8,128)(2,1)S(1)}, bf16[512,128]{1,0:T(8,128)(2,1)S(1)}) custom-call(f32[512,128]{1,0:T(8,128)S(1)} %bitcast.8, bf16[4,512,128]{2,1,0:T(8,128)(2,1)S(1)} %bitcast.7, bf16[8,64,448]{2,1,0:T(8,128)(2,1)S(1)} %copy-done.1, s32[8,6]{1,0:T(8,128)S(1)} %copy-done.4, f32[8,64]{1,0:T(8,128)S(1)} %copy-done.5, ...), custom_call_target="tpu_custom_call" | custom-call | tf_op jit(solution)/shard_map/pallas_call | solution.py:345
  172.8 1.1 convert.2
  173.9 0.7 convert.3
Async XLA Ops:
  0.6 1.0 copy-start
  1.7 1.0 copy-start.1
  2.7 0.9 copy-start.2
  3.7 0.8 copy-start.3
  4.4 0.7 copy-start.4
  5.1 0.7 copy-start.5
where the time goes:
time: 176 us; the launch traced here: 175 us
  Pallas kernels  167 us (95%)
  local copies, waits for them, and re-layouts  5.16 us (3%)
  other arithmetic  1.8 us (1%)
    pallas_call x1, Pallas kernels, body(): pl.pallas_call(kernel, out_shape=(jax.ShapeDtypeStruct((STEPS, ROWS, ENS)...  167 us
    unnamed x12, local copies, waits for them, and re-layouts  5.16 us

commit v1 on v0

v1 whole, which is shorter than its diff:
```python
import functools

import jax
import jax.numpy as jnp
from jax import lax
from jax.experimental import pallas as pl
from jax.experimental.pallas import tpu as pltpu
from jax.sharding import PartitionSpec as P

BRICK = 64
ENS = 128
NB = 6
REACH = 4
Q = 8
STEPS = 4
ITERS = 2
HERE = 8
SLICES = 32
ROWS = HERE * BRICK
HALF = ROWS // 2

MESH = pl.DeviceIdType.MESH
HIGHEST = lax.Precision.HIGHEST
F32 = jnp.float32
BF16 = jnp.bfloat16


def dot(a, b):
    return jnp.dot(a, b, preferred_element_type=F32)


def dot32(a, b):
    return jnp.dot(a, b, preferred_element_type=F32, precision=HIGHEST)


def kernel(
    init_ref, forcing_ref, blocks_ref, neighbours_ref, modes_ref, coarse_ref,
    sol_ref, def_ref,
    fields, weights, home_nbr, nbr, start, state, columns, band, diag, ext00, ext01, ext10, ext11,
    restrict, strip, toep_high, toep_low, r_buf, in0, in1, err0, err1, got0, got1, all0, all1,
    powers, held, stage,
    field_sem, weight_sem, nbr_sem, start_sem, halo_send, halo_recv, swap_send,
    sc_send, sc_recv, all_send, all_recv, power_send, power_recv, out_send, sol_recv, def_recv,
):
    tm = lax.axis_index("tm")
    sp = lax.axis_index("space")
    c = lax.rem(tm, 2)
    zl = lax.rem(tm // 2, 4)
    x = tm // 8
    y = sp // 2
    zh = lax.rem(sp, 2)
    keeps = c == zh
    moves = c != zh
    j = x * 8 + zl * 2 + zh
    q = 2 * y + c
    partner = (tm - c + zh, sp - zh + c)
    q_low = lax.rem(q + 7, 8)
    q_high = lax.rem(q + 1, 8)
    low = (tm - c + lax.rem(q_low, 2), (q_low // 2) * 2 + zh)
    high = (tm - c + lax.rem(q_high, 2), (q_high // 2) * 2 + zh)

    def worker(slice_id):
        return (
            (slice_id // 8) * 8 + lax.rem(slice_id // 2, 4) * 2 + c,
            2 * y + lax.rem(slice_id, 2),
        )

    def in_plane(other):
        return (tm - c + lax.rem(other, 2), (other // 2) * 2 + zh)

    @pl.when(keeps)
    def _():
        pltpu.make_async_copy(blocks_ref, weights, weight_sem).start()
        for i in range(STEPS):
            pltpu.make_async_copy(forcing_ref.at[i], fields.at[i], field_sem.at[i]).start()

    barrier = pltpu.get_barrier_semaphore()

    @pl.when(moves)
    def _():
        pl.semaphore_signal(barrier, inc=1, device_id=partner, device_id_type=MESH)

    @pl.loop(1, HERE)
    def _(d):
        pl.semaphore_signal(
            barrier, inc=1, device_id=in_plane(lax.rem(q + d, HERE)), device_id_type=MESH
        )

    @pl.loop(1, SLICES)
    def _(d):
        pl.semaphore_signal(
            barrier, inc=1, device_id=worker(lax.rem(j + d, SLICES)), device_id_type=MESH
        )

    home_nbr[...] = jnp.zeros_like(home_nbr)
    home_nbr[:, 0:NB] = neighbours_ref[...]
    peers = SLICES - 1 + HERE - 1
    pl.semaphore_wait(barrier, jnp.where(moves, peers + 1, peers))

    def remote(src, dst, send, recv, device):
        return pltpu.make_async_remote_copy(
            src_ref=src, dst_ref=dst, send_sem=send, recv_sem=recv,
            device_id=device, device_id_type=MESH,
        )

    def arrived(ref, sem):
        pltpu.make_async_copy(ref, ref, sem).wait()

    @pl.when(keeps)
    def _():
        pltpu.make_async_copy(home_nbr, nbr, nbr_sem).start()

    @pl.when(moves)
    def _():
        remote(home_nbr, nbr, swap_send.at[5], nbr_sem, partner).start()
        remote(blocks_ref, weights, swap_send.at[4], weight_sem, partner).start()
        for i in range(STEPS):
            remote(
                forcing_ref.at[i], fields.at[i], swap_send.at[i], field_sem.at[i], partner
            ).start()

    @pl.when((tm == 0) & (zh == 1))
    def _():
        remote(init_ref, start, swap_send.at[6], start_sem, partner).start()

    @pl.when((tm == 0) & (zh == 0))
    def _():
        pltpu.make_async_copy(init_ref, start, start_sem).start()

    modes = modes_ref[...]
    wide = jnp.concatenate([jnp.concatenate([modes] * 4, axis=1)] * 4, axis=0)
    row = lax.broadcasted_iota(jnp.int32, (4 * Q, HALF), 0)
    col = lax.broadcasted_iota(jnp.int32, (4 * Q, HALF), 1)
    restrict[...] = jnp.where(row // Q == col // BRICK, wide, 0.0)

    owns = keeps & (zl < 2)
    group = lax.rem(zl, 2)
    four = coarse_ref[pl.ds(4 * group, 4)].reshape(4 * Q, Q)
    row = lax.broadcasted_iota(jnp.int32, (4 * Q, 4 * Q), 0)
    col = lax.broadcasted_iota(jnp.int32, (4 * Q, 4 * Q), 1)
    power = jnp.where(row // Q == col // Q, jnp.concatenate([four] * 4, axis=1), 0.0)
    chain = (row == col).astype(F32)
    while chain.shape[1] < SLICES * 4 * Q:
        chain = jnp.concatenate([dot32(power, chain), chain], axis=1)
        power = dot32(power, power)
    strip[:, 0 : SLICES * 4 * Q] = chain
    strip[:, SLICES * 4 * Q :] = jnp.zeros((4 * Q, SLICES * 4 * Q), F32)
    near = strip[:, pl.ds(pl.multiple_of((3 - x) * 256, 256), 1280)]
    for d in range(9):
        first = (8 - d) * 4 * Q
        part = near[:, first : first + SLICES * 4 * Q]
        high_part = part.astype(BF16)
        toep_high[d * 4 * Q : (d + 1) * 4 * Q, :] = high_part
        toep_low[d * 4 * Q : (d + 1) * 4 * Q, :] = (part - high_part.astype(F32)).astype(BF16)

    tall = jnp.concatenate([modes] * 16, axis=0).T
    row = lax.broadcasted_iota(jnp.int32, (BRICK, ENS), 0) * 0 + 8 * c
    col = lax.broadcasted_iota(jnp.int32, (BRICK, ENS), 1) // Q
    for b in range(HERE):
        columns[b * BRICK : (b + 1) * BRICK, :] = jnp.where(
            (row + b == col) & (y == x), tall, 0.0
        )

    arrived(nbr, nbr_sem)
    arrived(weights, weight_sem)
    brick_ids = lax.broadcasted_iota(jnp.int32, (HERE, 128), 0)
    shift = lax.rem(nbr[...] - (8 * q + brick_ids) + (REACH + 64), 64)
    nbr[...] = shift + lax.rem(brick_ids, 4)
    lane_brick = lax.broadcasted_iota(jnp.int32, (BRICK, 128), 1) // BRICK

    @pl.loop(0, HERE)
    def _(b):
        g, b4 = b // 4, lax.rem(b, 4)
        rows = pl.ds(pl.multiple_of(b4 * BRICK, BRICK), BRICK)
        places = nbr[pl.ds(b, 1), :]
        where = [jnp.broadcast_to(places[:, k : k + 1], (BRICK, 128)) for k in range(NB)]
        twice = []
        for k in range(NB + 1):
            block = weights[b, :, k * BRICK : (k + 1) * BRICK].astype(F32)
            twice.append(jnp.concatenate([block, block], axis=1))
        for pair in range(6):
            there = lane_brick + 2 * pair
            block = jnp.zeros((BRICK, 128), F32)
            for k in range(NB):
                block = jnp.where(where[k] == there, twice[k + 1], block)
            band[g, rows, pair * 128 : (pair + 1) * 128] = block.astype(BF16)
        for pair in range(2):
            block = jnp.where(lane_brick + 2 * pair == b4, twice[0], 0.0)
            diag[g, rows, pair * 128 : (pair + 1) * 128] = block.astype(BF16)

    exts = ((ext00, ext01), (ext10, ext11))

    def halo(u, sweep):
        ext = exts[u][sweep]
        down = remote(
            ext.at[pl.ds(HALF, HALF)], ext.at[pl.ds(3 * HALF, HALF)],
            halo_send.at[u, sweep, 0], halo_recv.at[u, sweep, 0], low,
        )
        up = remote(
            ext.at[pl.ds(2 * HALF, HALF)], ext.at[pl.ds(0, HALF)],
            halo_send.at[u, sweep, 1], halo_recv.at[u, sweep, 1], high,
        )
        return down, up

    def begin(u, sweep, values):
        ext = exts[u][sweep]
        down, up = halo(u, sweep)
        ext[HALF : 2 * HALF, :] = dot(diag[0], values[0].astype(BF16)).astype(BF16)
        down.start()
        ext[2 * HALF : 3 * HALF, :] = dot(diag[1], values[1].astype(BF16)).astype(BF16)
        up.start()

    def end(u, sweep, values):
        ext = exts[u][sweep]
        near = (
            dot(band[0, :, HALF:], ext[HALF : 3 * HALF, :]),
            dot(band[1, :, : 2 * HALF], ext[HALF : 3 * HALF, :]),
        )
        down, up = halo(u, sweep)
        down.wait_send()
        up.wait_send()
        down.wait_recv()
        up.wait_recv()
        return (
            values[0] - near[0] - dot(band[0, :, :HALF], ext[0:HALF, :]),
            values[1] - near[1] - dot(band[1, :, 2 * HALF :], ext[3 * HALF :, :]),
        )

    def halves(g):
        return slice(g * HALF, (g + 1) * HALF)

    def deliver(n):
        target = sol_ref.at[n] if n < STEPS else def_ref

        @pl.when(keeps)
        def _():
            pltpu.make_async_copy(
                stage.at[n], target, sol_recv if n < STEPS else def_recv
            ).start()

        @pl.when(moves)
        def _():
            remote(
                stage.at[n], target, out_send.at[n], sol_recv if n < STEPS else def_recv, partner
            ).start()

    def share(i):
        for d in range(1, 4):
            remote(
                powers.at[i, x], powers.at[i, x], power_send.at[i], power_recv.at[i],
                (lax.rem(x + d, 4) * 8 + zl * 2 + c, sp),
            ).start()

    @pl.when(j == 0)
    def _():
        arrived(start, start_sem)
        state[...] = start[...]

    @pl.when(j != 0)
    def _():
        state[...] = jnp.zeros_like(state)

    @pl.loop(0, STEPS)
    def _(i):
        refs = (state, columns)

        def values(u):
            return refs[u][0:HALF, :], refs[u][HALF:ROWS, :]

        begin(0, 0, values(0))
        begin(1, 0, values(1))
        begin(0, 1, end(0, 0, values(0)))
        begin(1, 1, end(1, 0, values(1)))
        last = end(0, 1, values(0))
        arrived(fields.at[i], field_sem.at[i])
        for g in range(2):
            following = dot(diag[g], last[g].astype(BF16)) + fields[i, halves(g), :].astype(F32)
            state[halves(g), :] = following
            held[i, halves(g), :] = following
        last = end(1, 1, values(1))
        for g in range(2):
            following = dot(diag[g], last[g].astype(BF16))
            columns[halves(g), :] = following
            powers[i, x, halves(g), :] = following.astype(BF16)

        @pl.when(i < STEPS - 1)
        def _():
            share(i)

    prolong = restrict[...].T

    def coarse_part(i, gathered, g):
        matrix = jnp.concatenate([powers[i, n, halves(g), :] for n in range(4)], axis=1)
        return dot(matrix, gathered[...])

    sum_prev = sum_here = None
    for it, (incoming, err, got, gathered) in enumerate(
        ((in0, err0, got0, all0), (in1, err1, got1, all1))
    ):
        for g in range(2):
            defect = state[halves(g), :]
            if it:
                defect += coarse_part(STEPS - 1, all0, g)
                defect -= dot32(prolong, sum_here[g])
                stage[STEPS, halves(g), :] = defect.astype(BF16)
            r_buf[it, g] = dot32(restrict[...], defect).astype(BF16)

        @pl.loop(0, 8)
        def _(w):
            g = lax.rem(w, 2)
            owner_tm = (w // 2) * 8 + g * 2 + c
            owner_sp = 2 * y + c
            mine = (owner_tm == tm) & (owner_sp == sp)

            @pl.when(mine)
            def _():
                incoming[j] = r_buf[it, g]

            @pl.when(jnp.logical_not(mine))
            def _():
                remote(
                    r_buf.at[it, g], incoming.at[j], sc_send.at[it, 0], sc_recv.at[it, 0],
                    (owner_tm, owner_sp),
                ).start()

        if it:
            deliver(STEPS)
        else:
            share(STEPS - 1)

        @pl.when(owns)
        def _():
            arrived(incoming.at[pl.ds(0, SLICES - 1)], sc_recv.at[it, 0])
            terms = incoming[...].reshape(SLICES * 4 * Q, ENS)
            errors = dot(toep_high[...], terms) + dot(toep_low[...], terms)
            err[...] = errors.astype(BF16).reshape(9, 4 * Q, ENS)

            @pl.loop(0, 8)
            def _(d):
                there = x * 8 + d

                @pl.when(there == j)
                def _():
                    got[group] = err[pl.ds(d, 2)]

                @pl.when(there != j)
                def _():
                    remote(
                        err.at[pl.ds(d, 2)], got.at[group],
                        sc_send.at[it, 1], sc_recv.at[it, 1], worker(there),
                    ).start()

            arrived(got.at[0], sc_recv.at[it, 1])

        @pl.when(jnp.logical_not(owns))
        def _():
            arrived(got, sc_recv.at[it, 1])

        e_prev = [got[g, 0].astype(F32) for g in range(2)]
        e_here = [got[g, 1].astype(F32) for g in range(2)]
        if it:
            e_prev = [a + b for a, b in zip(e_prev, sum_prev)]
            e_here = [a + b for a, b in zip(e_here, sum_here)]
        sum_prev, sum_here = e_prev, e_here
        mine = pl.ds(pl.multiple_of(q * HERE * Q, HERE * Q), HERE * Q)
        gathered[mine, :] = jnp.concatenate(sum_prev, axis=0).astype(BF16)

        @pl.loop(1, HERE)
        def _(d):
            remote(
                gathered.at[mine], gathered.at[mine], all_send.at[it], all_recv.at[it],
                in_plane(lax.rem(q + d, HERE)),
            ).start()

        if it:
            for g in range(2):
                stage[STEPS - 1, halves(g), :] = dot32(prolong, sum_here[g]).astype(BF16)
            deliver(STEPS - 1)
        else:
            arrived(powers.at[STEPS - 1, pl.ds(0, 3)], power_recv.at[STEPS - 1])
        arrived(gathered.at[pl.ds(0, 7 * HERE * Q)], all_recv.at[it])

    for i in range(STEPS - 1):
        arrived(powers.at[i, pl.ds(0, 3)], power_recv.at[i])
        for g in range(2):
            stage[i, halves(g), :] = (held[i, halves(g), :] + coarse_part(i, all1, g)).astype(BF16)
        deliver(i)

    for it, (incoming, got) in enumerate(((in0, got0), (in1, got1))):
        arrived(all0.at[pl.ds(0, 7 * HERE * Q)], all_send.at[it])

        @pl.when(owns)
        def _():
            arrived(incoming.at[pl.ds(0, 7)], sc_send.at[it, 0])
            arrived(incoming.at[pl.ds(0, 14)], sc_send.at[it, 1])

        @pl.when(jnp.logical_not(owns))
        def _():
            arrived(incoming.at[pl.ds(0, 8)], sc_send.at[it, 0])

    for i in range(STEPS):
        arrived(powers.at[i, pl.ds(0, 3)], power_send.at[i])

    @pl.when(moves)
    def _():
        arrived(home_nbr, swap_send.at[5])
        arrived(weights, swap_send.at[4])
        for i in range(STEPS):
            arrived(fields.at[i], swap_send.at[i])
        for n in range(STEPS + 1):
            arrived(stage.at[n], out_send.at[n])

    @pl.when((tm == 0) & (zh == 1))
    def _():
        arrived(start, swap_send.at[6])

    arrived(sol_ref, sol_recv)
    arrived(def_ref, def_recv)


def body(initial, forcing, brick_blocks, neighbours, coarse_modes, coarse_blocks):
    vmem = pl.BlockSpec(memory_space=pltpu.VMEM)
    hbm = pl.BlockSpec(memory_space=pl.ANY)
    sem = pltpu.SemaphoreType.DMA
    sol, last = pl.pallas_call(
        kernel,
        out_shape=(
            jax.ShapeDtypeStruct((STEPS, ROWS, ENS), BF16),
            jax.ShapeDtypeStruct((ROWS, ENS), BF16),
        ),
        in_specs=[hbm, hbm, hbm, vmem, vmem, vmem],
        out_specs=(hbm, hbm),
        scratch_shapes=[
            pltpu.VMEM((STEPS, ROWS, ENS), BF16),
            pltpu.VMEM((HERE, BRICK, (NB + 1) * BRICK), BF16),
            pltpu.VMEM((HERE, 128), jnp.int32),
            pltpu.VMEM((HERE, 128), jnp.int32),
            pltpu.VMEM((ROWS, ENS), F32),
            pltpu.VMEM((ROWS, ENS), F32),
            pltpu.VMEM((ROWS, ENS), F32),
            pltpu.VMEM((2, HALF, 3 * HALF), BF16),
            pltpu.VMEM((2, HALF, HALF), BF16),
            *[pltpu.VMEM((4 * HALF, ENS), BF16)] * 4,
            pltpu.VMEM((4 * Q, HALF), F32),
            pltpu.VMEM((4 * Q, 2 * SLICES * 4 * Q), F32),
            pltpu.VMEM((9 * 4 * Q, SLICES * 4 * Q), BF16),
            pltpu.VMEM((9 * 4 * Q, SLICES * 4 * Q), BF16),
            pltpu.VMEM((ITERS, 2, 4 * Q, ENS), BF16),
            *[pltpu.VMEM((SLICES, 4 * Q, ENS), BF16)] * 2,
            *[pltpu.VMEM((9, 4 * Q, ENS), BF16)] * 2,
            *[pltpu.VMEM((2, 2, 4 * Q, ENS), BF16)] * 2,
            *[pltpu.VMEM((HERE * HERE * Q, ENS), BF16)] * 2,
            pltpu.VMEM((STEPS, 4, ROWS, ENS), BF16),
            pltpu.VMEM((STEPS, ROWS, ENS), F32),
            pltpu.VMEM((STEPS + 1, ROWS, ENS), BF16),
            sem((STEPS,)),
            sem,
            sem,
            sem,
            sem((2, 2, 2)),
            sem((2, 2, 2)),
            sem((7,)),
            sem((ITERS, 2)),
            sem((ITERS, 2)),
            sem((ITERS,)),
            sem((ITERS,)),
            sem((STEPS,)),
            sem((STEPS,)),
            sem((STEPS + 1,)),
            sem,
            sem,
        ],
        compiler_params=pltpu.CompilerParams(
            collective_id=0, has_side_effects=True, vmem_limit_bytes=60 * 2**20
        ),
    )(
        initial.reshape(ROWS, ENS),
        forcing.reshape(STEPS, ROWS, ENS),
        brick_blocks,
        neighbours,
        coarse_modes,
        coarse_blocks,
    )
    return (
        sol.astype(F32).reshape(STEPS, HERE, BRICK, ENS),
        last.astype(F32).reshape(1, HERE, BRICK, ENS),
    )


def solution(mesh):
    placed = (
        P("space", None, None),
        P("tm", "space", None, None),
        P("space", None, None),
        P("space", None),
        P(),
        P("space", None, None),
    )
    return jax.shard_map(
        body,
        mesh=mesh,
        in_specs=placed,
        out_specs=(P("tm", "space", None, None), P("tm", "space", None, None)),
        check_vma=False,
    )
```

time: 176 us -> 126 us (0.72)
  the two profiles are of different devices: /device:TPU:7 before, /device:TPU:37 now
where the time goes in v1:
time: 126 us
  Pallas kernels  122 us (97%)
  other arithmetic  2.88 us (2%)
    pallas_call x1, Pallas kernels, body(): pl.pallas_call(kernel, out_shape=(jax.ShapeDtypeStruct((STEPS, ROWS, ENS)...  122 us

profile of v1, /device:TPU:37, one launch (start us, length us, event | category | flops | bytes accessed | tf_op | source)
XLA Modules:
  0.0 125.9 jit_solution(12729417065841807245)
XLA Ops:
  0.6 122.3 %shard_map.77 = (bf16[4,512,128]{2,1,0:T(8,128)(2,1)}, bf16[512,128]{1,0:T(8,128)(2,1)}) custom-call(f32[512,128]{1,0:T(8,128)} %bitcast.8, bf16[4,512,128]{2,1,0:T(8,128)(2,1)} %bitcast.7, bf16[8,64,448]{2,1,0:T(8,128)(2,1)} %blocks_ref.1, s32[8,6]{1,0:T(8,128)} %neighbours_ref.1, f32[8,64]{1,0:T(8,128)} %modes_ref.1, f32[8,8,8]{2,1,0:T(8,128)} %coarse_ref.1), custom_call_target="tpu_custom_call" | custom-call | tf_op jit(solution)/shard_map/pallas_call | solution.py:425
  123.0 0.0 copy-start
  123.0 2.2 %convert.2 = f32[4,8,64,128]{3,2,1,0:T(8,128)} convert(bf16[4,8,64,128]{3,2,1,0:T(8,128)(2,1)} %bitcast.6) | non-fusion elementwise | flops 262144 | bytes 1572864 | tf_op jit(solution)/shard_map/reshape | solution.py:485
  125.1 0.0 copy-done
  125.2 0.7 convert.3
Async XLA Ops:
  123.0 2.2 %copy-start = (bf16[512,128]{1,0:T(8,128)(2,1)S(1)}, bf16[512,128]{1,0:T(8,128)(2,1)}, u32[]{:S(2)}) copy-start(bf16[512,128]{1,0:T(8,128)(2,1)} %get-tuple-element.5) | copy-start | bytes 393220

commit v2 on v1

--- a/solution.py
+++ b/solution.py
@@ -39,7 +39,7 @@
     fields, weights, home_nbr, nbr, start, state, columns, band, diag, ext00, ext01, ext10, ext11,
     restrict, strip, toep_high, toep_low, r_buf, in0, in1, err0, err1, got0, got1, all0, all1,
     powers, held, stage,
-    field_sem, weight_sem, nbr_sem, start_sem, halo_send, halo_recv, swap_send,
+    field_sem, weight_sem, nbr_sem, start_sem, halo_send, halo_recv, swap_send, row_send, row_recv,
     sc_send, sc_recv, all_send, all_recv, power_send, power_recv, out_send, sol_recv, def_recv,
 ):
     tm = lax.axis_index("tm")
@@ -54,10 +54,7 @@
     j = x * 8 + zl * 2 + zh
     q = 2 * y + c
     partner = (tm - c + zh, sp - zh + c)
-    q_low = lax.rem(q + 7, 8)
-    q_high = lax.rem(q + 1, 8)
-    low = (tm - c + lax.rem(q_low, 2), (q_low // 2) * 2 + zh)
-    high = (tm - c + lax.rem(q_high, 2), (q_high // 2) * 2 + zh)
+    slow, fast = c, 1 - c
 
     def worker(slice_id):
         return (
@@ -110,14 +107,19 @@
     def _():
         pltpu.make_async_copy(home_nbr, nbr, nbr_sem).start()
 
+    def field(i):
+        return remote(
+            forcing_ref.at[i], fields.at[i], swap_send.at[i], field_sem.at[i], partner
+        )
+
+    fetched = pl.ds(2 * x, 2)
+
     @pl.when(moves)
     def _():
         remote(home_nbr, nbr, swap_send.at[5], nbr_sem, partner).start()
-        remote(blocks_ref, weights, swap_send.at[4], weight_sem, partner).start()
-        for i in range(STEPS):
-            remote(
-                forcing_ref.at[i], fields.at[i], swap_send.at[i], field_sem.at[i], partner
-            ).start()
+        remote(
+            blocks_ref.at[fetched], weights.at[fetched], swap_send.at[4], weight_sem, partner
+        ).start()
 
     @pl.when((tm == 0) & (zh == 1))
     def _():
@@ -162,10 +164,27 @@
         )
 
     arrived(nbr, nbr_sem)
-    arrived(weights, weight_sem)
+
+    @pl.when(keeps)
+    def _():
+        arrived(weights, weight_sem)
+
+    @pl.when(moves)
+    def _():
+        arrived(weights.at[pl.ds(0, 2)], weight_sem)
+        for d in range(1, 4):
+            remote(
+                weights.at[fetched], weights.at[fetched], row_send, row_recv,
+                (lax.rem(x + d, 4) * 8 + zl * 2 + c, sp),
+            ).start()
+        field(0).start()
+        field(1).start()
+        arrived(weights.at[pl.ds(0, 6)], row_recv)
+
     brick_ids = lax.broadcasted_iota(jnp.int32, (HERE, 128), 0)
     shift = lax.rem(nbr[...] - (8 * q + brick_ids) + (REACH + 64), 64)
-    nbr[...] = shift + lax.rem(brick_ids, 4)
+    window = shift + lax.rem(brick_ids, 4)
+    nbr[...] = jnp.where(brick_ids < 4, lax.rem(window + 8, 12), window)
     lane_brick = lax.broadcasted_iota(jnp.int32, (BRICK, 128), 1) // BRICK
 
     @pl.loop(0, HERE)
@@ -190,41 +209,27 @@
 
     exts = ((ext00, ext01), (ext10, ext11))
 
-    def halo(u, sweep):
+    def rows_of(g):
+        return pl.ds(pl.multiple_of(g * HALF, HALF), HALF)
+
+    def halo(u, sweep, g):
         ext = exts[u][sweep]
-        down = remote(
-            ext.at[pl.ds(HALF, HALF)], ext.at[pl.ds(3 * HALF, HALF)],
-            halo_send.at[u, sweep, 0], halo_recv.at[u, sweep, 0], low,
-        )
-        up = remote(
-            ext.at[pl.ds(2 * HALF, HALF)], ext.at[pl.ds(0, HALF)],
-            halo_send.at[u, sweep, 1], halo_recv.at[u, sweep, 1], high,
-        )
-        return down, up
-
-    def begin(u, sweep, values):
+        return remote(
+            ext.at[rows_of(g)], ext.at[rows_of(3 - g)],
+            halo_send.at[u, sweep, g], halo_recv.at[u, sweep, 1 - g],
+            in_plane(lax.rem(q + 7 + 2 * g, HERE)),
+        )
+
+    def send_half(u, sweep, g, values):
+        exts[u][sweep][rows_of(g), :] = dot(diag[g], values.astype(BF16)).astype(BF16)
+        halo(u, sweep, g).start()
+
+    def uncoupled(u, sweep, g):
         ext = exts[u][sweep]
-        down, up = halo(u, sweep)
-        ext[HALF : 2 * HALF, :] = dot(diag[0], values[0].astype(BF16)).astype(BF16)
-        down.start()
-        ext[2 * HALF : 3 * HALF, :] = dot(diag[1], values[1].astype(BF16)).astype(BF16)
-        up.start()
-
-    def end(u, sweep, values):
-        ext = exts[u][sweep]
-        near = (
-            dot(band[0, :, HALF:], ext[HALF : 3 * HALF, :]),
-            dot(band[1, :, : 2 * HALF], ext[HALF : 3 * HALF, :]),
-        )
-        down, up = halo(u, sweep)
-        down.wait_send()
-        up.wait_send()
-        down.wait_recv()
-        up.wait_recv()
-        return (
-            values[0] - near[0] - dot(band[0, :, :HALF], ext[0:HALF, :]),
-            values[1] - near[1] - dot(band[1, :, 2 * HALF :], ext[3 * HALF :, :]),
-        )
+        near = dot(band[g, :, : 2 * HALF], ext[0 : 2 * HALF, :])
+        arrived(ext.at[rows_of(2 + g)], halo_recv.at[u, sweep, g])
+        far = dot(band[g, :, 2 * HALF :], ext[rows_of(2 + g), :])
+        return (state, columns)[u][rows_of(g), :] - near - far
 
     def halves(g):
         return slice(g * HALF, (g + 1) * HALF)
@@ -260,28 +265,36 @@
     def _():
         state[...] = jnp.zeros_like(state)
 
+    for u, ref in enumerate((state, columns)):
+        for g in (slow, fast):
+            send_half(u, 0, g, ref[rows_of(g), :])
+
     @pl.loop(0, STEPS)
     def _(i):
-        refs = (state, columns)
-
-        def values(u):
-            return refs[u][0:HALF, :], refs[u][HALF:ROWS, :]
-
-        begin(0, 0, values(0))
-        begin(1, 0, values(1))
-        begin(0, 1, end(0, 0, values(0)))
-        begin(1, 1, end(1, 0, values(1)))
-        last = end(0, 1, values(0))
+        @pl.when(moves & (i < 2))
+        def _():
+            field(i + 2).start()
+
+        for g in (fast, slow):
+            for u in range(2):
+                send_half(u, 1, g, uncoupled(u, 0, g))
         arrived(fields.at[i], field_sem.at[i])
-        for g in range(2):
-            following = dot(diag[g], last[g].astype(BF16)) + fields[i, halves(g), :].astype(F32)
-            state[halves(g), :] = following
-            held[i, halves(g), :] = following
-        last = end(1, 1, values(1))
-        for g in range(2):
-            following = dot(diag[g], last[g].astype(BF16))
-            columns[halves(g), :] = following
-            powers[i, x, halves(g), :] = following.astype(BF16)
+        for g in (fast, slow):
+            for u in range(2):
+                following = dot(diag[g], uncoupled(u, 1, g).astype(BF16))
+                arrived(ext00.at[rows_of(0)], halo_send.at[u, 0, g])
+                arrived(ext00.at[rows_of(0)], halo_send.at[u, 1, g])
+                if u == 0:
+                    following += fields[i, rows_of(g), :].astype(F32)
+                    state[rows_of(g), :] = following
+                    held[i, rows_of(g), :] = following
+                else:
+                    columns[rows_of(g), :] = following
+                    powers[i, x, rows_of(g), :] = following.astype(BF16)
+
+                @pl.when(i < STEPS - 1)
+                def _():
+                    send_half(u, 0, g, following)
 
         @pl.when(i < STEPS - 1)
         def _():
@@ -404,7 +417,8 @@
     @pl.when(moves)
     def _():
         arrived(home_nbr, swap_send.at[5])
-        arrived(weights, swap_send.at[4])
+        arrived(weights.at[pl.ds(0, 2)], swap_send.at[4])
+        arrived(weights.at[pl.ds(0, 6)], row_send)
         for i in range(STEPS):
             arrived(fields.at[i], swap_send.at[i])
         for n in range(STEPS + 1):
@@ -460,6 +474,8 @@
             sem((2, 2, 2)),
             sem((2, 2, 2)),
             sem((7,)),
+            sem,
+            sem,
             sem((ITERS, 2)),
             sem((ITERS, 2)),
             sem((ITERS,)),

time: 126 us -> 109 us (0.87)
  the two profiles are of different devices: /device:TPU:37 before, /device:TPU:7 now
where the time goes in v2:
time: 109 us
  Pallas kernels  106 us (97%)
  other arithmetic  2.88 us (3%)
    pallas_call x1, Pallas kernels, body(): pl.pallas_call(kernel, out_shape=(jax.ShapeDtypeStruct((STEPS, ROWS, ENS)...  106 us

profile of v2, /device:TPU:7, one launch (start us, length us, event | category | flops | bytes accessed | tf_op | source)
XLA Modules:
  0.0 109.2 jit_solution(8755847638568928920)
XLA Ops:
  0.6 105.7 %shard_map.77 = (bf16[4,512,128]{2,1,0:T(8,128)(2,1)}, bf16[512,128]{1,0:T(8,128)(2,1)}) custom-call(f32[512,128]{1,0:T(8,128)} %bitcast.8, bf16[4,512,128]{2,1,0:T(8,128)(2,1)} %bitcast.7, bf16[8,64,448]{2,1,0:T(8,128)(2,1)} %blocks_ref.1, s32[8,6]{1,0:T(8,128)} %neighbours_ref.1, f32[8,64]{1,0:T(8,128)} %modes_ref.1, f32[8,8,8]{2,1,0:T(8,128)} %coarse_ref.1), custom_call_target="tpu_custom_call" | custom-call | tf_op jit(solution)/shard_map/pallas_call | solution.py:439
  106.3 0.0 copy-start
  106.3 2.2 %convert.2 = f32[4,8,64,128]{3,2,1,0:T(8,128)} convert(bf16[4,8,64,128]{3,2,1,0:T(8,128)(2,1)} %bitcast.6) | non-fusion elementwise | flops 262144 | bytes 1572864 | tf_op jit(solution)/shard_map/reshape | solution.py:501
  108.5 0.0 copy-done
  108.5 0.7 convert.3
Async XLA Ops:
  106.3 2.2 %copy-start = (bf16[512,128]{1,0:T(8,128)(2,1)S(1)}, bf16[512,128]{1,0:T(8,128)(2,1)}, u32[]{:S(2)}) copy-start(bf16[512,128]{1,0:T(8,128)(2,1)} %get-tuple-element.5) | copy-start | bytes 393220

commit v3 on v2

--- a/solution.py
+++ b/solution.py
@@ -38,9 +38,10 @@
     sol_ref, def_ref,
     fields, weights, home_nbr, nbr, start, state, columns, band, diag, ext00, ext01, ext10, ext11,
     restrict, strip, toep_high, toep_low, r_buf, in0, in1, err0, err1, got0, got1, all0, all1,
-    powers, held, stage,
+    powers, home_powers, held, home_held, prev_buf, here_buf, home_here, stage,
     field_sem, weight_sem, nbr_sem, start_sem, halo_send, halo_recv, swap_send, row_send, row_recv,
-    sc_send, sc_recv, all_send, all_recv, power_send, power_recv, out_send, sol_recv, def_recv,
+    sc_send, sc_recv, all_send, all_recv, power_send, power_recv, forward_send, home_power_sem,
+    held_send, home_held_sem, here_send, here_recv, out_send, sol_recv, def_recv,
 ):
     tm = lax.axis_index("tm")
     sp = lax.axis_index("space")
@@ -75,7 +76,14 @@
 
     @pl.when(moves)
     def _():
-        pl.semaphore_signal(barrier, inc=1, device_id=partner, device_id_type=MESH)
+        @pl.loop(0, HERE)
+        def _(other):
+            pl.semaphore_signal(
+                barrier,
+                inc=1,
+                device_id=(tm - c + lax.rem(other, 2), (other // 2) * 2 + c),
+                device_id_type=MESH,
+            )
 
     @pl.loop(1, HERE)
     def _(d):
@@ -91,8 +99,7 @@
 
     home_nbr[...] = jnp.zeros_like(home_nbr)
     home_nbr[:, 0:NB] = neighbours_ref[...]
-    peers = SLICES - 1 + HERE - 1
-    pl.semaphore_wait(barrier, jnp.where(moves, peers + 1, peers))
+    pl.semaphore_wait(barrier, SLICES - 1 + HERE - 1 + HERE // 2)
 
     def remote(src, dst, send, recv, device):
         return pltpu.make_async_remote_copy(
@@ -234,27 +241,29 @@
     def halves(g):
         return slice(g * HALF, (g + 1) * HALF)
 
-    def deliver(n):
-        target = sol_ref.at[n] if n < STEPS else def_ref
-
-        @pl.when(keeps)
-        def _():
-            pltpu.make_async_copy(
-                stage.at[n], target, sol_recv if n < STEPS else def_recv
-            ).start()
-
-        @pl.when(moves)
-        def _():
-            remote(
-                stage.at[n], target, out_send.at[n], sol_recv if n < STEPS else def_recv, partner
-            ).start()
-
     def share(i):
         for d in range(1, 4):
             remote(
                 powers.at[i, x], powers.at[i, x], power_send.at[i], power_recv.at[i],
                 (lax.rem(x + d, 4) * 8 + zl * 2 + c, sp),
             ).start()
+
+    def forward(i):
+        arrived(powers.at[i, pl.ds(0, 3)], power_recv.at[i])
+        pltpu.make_async_copy(powers.at[i], home_powers.at[i], home_power_sem.at[i]).start()
+        remote(
+            powers.at[i], home_powers.at[i], forward_send.at[i], home_power_sem.at[i],
+            (tm - c + (1 - c), sp),
+        ).start()
+
+    def bring(source, target, send, recv):
+        @pl.when(keeps)
+        def _():
+            pltpu.make_async_copy(source, target, recv).start()
+
+        @pl.when(moves)
+        def _():
+            remote(source, target, send, recv, partner).start()
 
     @pl.when(j == 0)
     def _():
@@ -287,7 +296,7 @@
                 if u == 0:
                     following += fields[i, rows_of(g), :].astype(F32)
                     state[rows_of(g), :] = following
-                    held[i, rows_of(g), :] = following
+                    held[i, rows_of(g), :] = following.astype(BF16)
                 else:
                     columns[rows_of(g), :] = following
                     powers[i, x, rows_of(g), :] = following.astype(BF16)
@@ -298,12 +307,20 @@
 
         @pl.when(i < STEPS - 1)
         def _():
+            bring(held.at[i], home_held.at[i], held_send.at[i], home_held_sem.at[i])
+
+        @pl.when((i < STEPS - 1) & keeps)
+        def _():
             share(i)
 
+        @pl.when((i > 0) & keeps)
+        def _():
+            forward(i - 1)
+
     prolong = restrict[...].T
 
-    def coarse_part(i, gathered, g):
-        matrix = jnp.concatenate([powers[i, n, halves(g), :] for n in range(4)], axis=1)
+    def coarse_part(ref, i, gathered, g):
+        matrix = jnp.concatenate([ref[i, n, halves(g), :] for n in range(4)], axis=1)
         return dot(matrix, gathered[...])
 
     sum_prev = sum_here = None
@@ -313,7 +330,7 @@
         for g in range(2):
             defect = state[halves(g), :]
             if it:
-                defect += coarse_part(STEPS - 1, all0, g)
+                defect += coarse_part(powers, STEPS - 1, all0, g)
                 defect -= dot32(prolong, sum_here[g])
                 stage[STEPS, halves(g), :] = defect.astype(BF16)
             r_buf[it, g] = dot32(restrict[...], defect).astype(BF16)
@@ -337,7 +354,7 @@
                 ).start()
 
         if it:
-            deliver(STEPS)
+            bring(stage.at[STEPS], def_ref, out_send, def_recv)
         else:
             share(STEPS - 1)
 
@@ -376,31 +393,63 @@
             e_here = [a + b for a, b in zip(e_here, sum_here)]
         sum_prev, sum_here = e_prev, e_here
         mine = pl.ds(pl.multiple_of(q * HERE * Q, HERE * Q), HERE * Q)
-        gathered[mine, :] = jnp.concatenate(sum_prev, axis=0).astype(BF16)
-
-        @pl.loop(1, HERE)
-        def _(d):
-            remote(
-                gathered.at[mine], gathered.at[mine], all_send.at[it], all_recv.at[it],
-                in_plane(lax.rem(q + d, HERE)),
-            ).start()
-
-        if it:
-            for g in range(2):
-                stage[STEPS - 1, halves(g), :] = dot32(prolong, sum_here[g]).astype(BF16)
-            deliver(STEPS - 1)
+        rounded_prev = jnp.concatenate(sum_prev, axis=0).astype(BF16)
+        if it == 0:
+            gathered[mine, :] = rounded_prev
+
+            @pl.loop(1, HERE)
+            def _(d):
+                remote(
+                    gathered.at[mine], gathered.at[mine], all_send.at[it], all_recv.at[it],
+                    in_plane(lax.rem(q + d, HERE)),
+                ).start()
+
+            arrived(powers.at[STEPS - 1, pl.ds(0, 3)], power_recv.at[STEPS - 1])
+            arrived(gathered.at[pl.ds(0, 7 * HERE * Q)], all_recv.at[it])
         else:
-            arrived(powers.at[STEPS - 1, pl.ds(0, 3)], power_recv.at[STEPS - 1])
-        arrived(gathered.at[pl.ds(0, 7 * HERE * Q)], all_recv.at[it])
+            prev_buf[...] = rounded_prev
+            here_buf[...] = jnp.concatenate(sum_here, axis=0).astype(BF16)
+
+            @pl.loop(0, HERE)
+            def _(d):
+                home = lax.rem(sp + d, HERE)
+                own = keeps & (home == sp)
+
+                @pl.when(own)
+                def _():
+                    gathered[mine, :] = prev_buf[...]
+
+                @pl.when(jnp.logical_not(own))
+                def _():
+                    remote(
+                        prev_buf, gathered.at[mine], all_send.at[it], all_recv.at[it],
+                        (tm - c + zh, home),
+                    ).start()
+
+            bring(here_buf, home_here, here_send, here_recv)
+
+    @pl.when(keeps)
+    def _():
+        arrived(all1.at[pl.ds(0, 7 * HERE * Q)], all_recv.at[1])
+
+    @pl.when(moves)
+    def _():
+        arrived(all1, all_recv.at[1])
 
     for i in range(STEPS - 1):
-        arrived(powers.at[i, pl.ds(0, 3)], power_recv.at[i])
+        arrived(home_held.at[i], home_held_sem.at[i])
+        arrived(home_powers.at[i], home_power_sem.at[i])
         for g in range(2):
-            stage[i, halves(g), :] = (held[i, halves(g), :] + coarse_part(i, all1, g)).astype(BF16)
-        deliver(i)
-
-    for it, (incoming, got) in enumerate(((in0, got0), (in1, got1))):
-        arrived(all0.at[pl.ds(0, 7 * HERE * Q)], all_send.at[it])
+            value = home_held[i, halves(g), :].astype(F32) + coarse_part(home_powers, i, all1, g)
+            stage[i, halves(g), :] = value.astype(BF16)
+        pltpu.make_async_copy(stage.at[i], sol_ref.at[i], sol_recv).start()
+    arrived(home_here, here_recv)
+    for g in range(2):
+        part = home_here[g * 4 * Q : (g + 1) * 4 * Q, :].astype(F32)
+        stage[STEPS - 1, halves(g), :] = dot32(prolong, part).astype(BF16)
+    pltpu.make_async_copy(stage.at[STEPS - 1], sol_ref.at[STEPS - 1], sol_recv).start()
+
+    for it, incoming in enumerate((in0, in1)):
 
         @pl.when(owns)
         def _():
@@ -411,18 +460,28 @@
         def _():
             arrived(incoming.at[pl.ds(0, 8)], sc_send.at[it, 0])
 
-    for i in range(STEPS):
-        arrived(powers.at[i, pl.ds(0, 3)], power_send.at[i])
+    arrived(all0.at[pl.ds(0, 7 * HERE * Q)], all_send.at[0])
+    arrived(powers.at[STEPS - 1, pl.ds(0, 3)], power_send.at[STEPS - 1])
+
+    @pl.when(keeps)
+    def _():
+        arrived(all0.at[pl.ds(0, 7 * HERE * Q)], all_send.at[1])
+        for i in range(STEPS - 1):
+            arrived(powers.at[i, pl.ds(0, 3)], power_send.at[i])
+            arrived(powers.at[i], forward_send.at[i])
 
     @pl.when(moves)
     def _():
+        arrived(all0, all_send.at[1])
         arrived(home_nbr, swap_send.at[5])
         arrived(weights.at[pl.ds(0, 2)], swap_send.at[4])
         arrived(weights.at[pl.ds(0, 6)], row_send)
         for i in range(STEPS):
             arrived(fields.at[i], swap_send.at[i])
-        for n in range(STEPS + 1):
-            arrived(stage.at[n], out_send.at[n])
+        for i in range(STEPS - 1):
+            arrived(held.at[i], held_send.at[i])
+        arrived(stage.at[STEPS], out_send)
+        arrived(here_buf, here_send)
 
     @pl.when((tm == 0) & (zh == 1))
     def _():
@@ -465,7 +524,10 @@
             *[pltpu.VMEM((2, 2, 4 * Q, ENS), BF16)] * 2,
             *[pltpu.VMEM((HERE * HERE * Q, ENS), BF16)] * 2,
             pltpu.VMEM((STEPS, 4, ROWS, ENS), BF16),
-            pltpu.VMEM((STEPS, ROWS, ENS), F32),
+            pltpu.VMEM((STEPS - 1, 4, ROWS, ENS), BF16),
+            pltpu.VMEM((STEPS, ROWS, ENS), BF16),
+            pltpu.VMEM((STEPS - 1, ROWS, ENS), BF16),
+            *[pltpu.VMEM((HERE * Q, ENS), BF16)] * 3,
             pltpu.VMEM((STEPS + 1, ROWS, ENS), BF16),
             sem((STEPS,)),
             sem,
@@ -482,7 +544,13 @@
             sem((ITERS,)),
             sem((STEPS,)),
             sem((STEPS,)),
-            sem((STEPS + 1,)),
+            sem((STEPS - 1,)),
+            sem((STEPS - 1,)),
+            sem((STEPS - 1,)),
+            sem((STEPS - 1,)),
+            sem,
+            sem,
+            sem,
             sem,
             sem,
         ],

time: 109 us -> 100 us (0.917)
  Pallas kernels: 106 us -> 96.7 us
    pallas_call x1, Pallas kernels: 106 us -> 96.7 us  [body(): pl.pallas_call(kernel, out_shape=(jax.ShapeDtypeStruct((STEPS, ROWS, ENS)...]
where the time goes in v3:
time: 100 us
  Pallas kernels  96.7 us (97%)
  other arithmetic  2.88 us (3%)
    pallas_call x1, Pallas kernels, body(): pl.pallas_call(kernel, out_shape=(jax.ShapeDtypeStruct((STEPS, ROWS, ENS)...  96.7 us
    reshape x1, other arithmetic, body(): sol.astype(F32).reshape(STEPS, HERE, BRICK, ENS)  2.16 us

profile of v3, /device:TPU:7, one launch (start us, length us, event | category | flops | bytes accessed | tf_op | source)
XLA Modules:
  0.0 100.3 jit_solution(17981814634436420596)
XLA Ops:
  0.6 96.7 %shard_map.77 = (bf16[4,512,128]{2,1,0:T(8,128)(2,1)}, bf16[512,128]{1,0:T(8,128)(2,1)}) custom-call(f32[512,128]{1,0:T(8,128)} %bitcast.8, bf16[4,512,128]{2,1,0:T(8,128)(2,1)} %bitcast.7, bf16[8,64,448]{2,1,0:T(8,128)(2,1)} %blocks_ref.1, s32[8,6]{1,0:T(8,128)} %neighbours_ref.1, f32[8,64]{1,0:T(8,128)} %modes_ref.1, f32[8,8,8]{2,1,0:T(8,128)} %coarse_ref.1), custom_call_target="tpu_custom_call" | custom-call | tf_op jit(solution)/shard_map/pallas_call | solution.py:498
  97.4 0.0 copy-start
  97.4 2.2 %convert.2 = f32[4,8,64,128]{3,2,1,0:T(8,128)} convert(bf16[4,8,64,128]{3,2,1,0:T(8,128)(2,1)} %bitcast.6) | non-fusion elementwise | flops 262144 | bytes 1572864 | tf_op jit(solution)/shard_map/reshape | solution.py:569
  99.5 0.0 copy-done
  99.6 0.7 convert.3
Async XLA Ops:
  97.4 2.2 %copy-start = (bf16[512,128]{1,0:T(8,128)(2,1)S(1)}, bf16[512,128]{1,0:T(8,128)(2,1)}, u32[]{:S(2)}) copy-start(bf16[512,128]{1,0:T(8,128)(2,1)} %get-tuple-element.5) | copy-start | bytes 393220

commit v4 on v3

--- a/solution.py
+++ b/solution.py
@@ -36,10 +36,10 @@
 def kernel(
     init_ref, forcing_ref, blocks_ref, neighbours_ref, modes_ref, coarse_ref,
     sol_ref, def_ref,
-    fields, weights, home_nbr, nbr, start, state, columns, band, diag, ext00, ext01, ext10, ext11,
-    restrict, strip, toep_high, toep_low, r_buf, in0, in1, err0, err1, got0, got1, all0, all1,
+    fields, weights, home_nbr, nbr, start, state, columns, band, folded, diag, ext00, ext01, ext10, ext11,
+    restrict, prolong, strip, toep_high, toep_low, r_buf, in0, in1, err0, err1, got0, got1, all0, all1,
     powers, home_powers, held, home_held, prev_buf, here_buf, home_here, stage,
-    field_sem, weight_sem, nbr_sem, start_sem, halo_send, halo_recv, swap_send, row_send, row_recv,
+    field_sem, weight_sem, far_sem, nbr_sem, start_sem, halo_send, halo_recv, swap_send, row_send, row_recv,
     sc_send, sc_recv, all_send, all_recv, power_send, power_recv, forward_send, home_power_sem,
     held_send, home_held_sem, here_send, here_recv, out_send, sol_recv, def_recv,
 ):
@@ -120,6 +120,7 @@
         )
 
     fetched = pl.ds(2 * x, 2)
+    opposite = pl.ds(2 * lax.rem(x + 2, 4), 2)
 
     @pl.when(moves)
     def _():
@@ -127,6 +128,10 @@
         remote(
             blocks_ref.at[fetched], weights.at[fetched], swap_send.at[4], weight_sem, partner
         ).start()
+        arrived(weights.at[pl.ds(0, 2)], swap_send.at[4])
+        remote(
+            blocks_ref.at[opposite], weights.at[opposite], swap_send.at[7], far_sem, partner
+        ).start()
 
     @pl.when((tm == 0) & (zh == 1))
     def _():
@@ -140,27 +145,44 @@
     wide = jnp.concatenate([jnp.concatenate([modes] * 4, axis=1)] * 4, axis=0)
     row = lax.broadcasted_iota(jnp.int32, (4 * Q, HALF), 0)
     col = lax.broadcasted_iota(jnp.int32, (4 * Q, HALF), 1)
-    restrict[...] = jnp.where(row // Q == col // BRICK, wide, 0.0)
+    wide = jnp.where(row // Q == col // BRICK, wide, 0.0)
+    wide_high = wide.astype(BF16)
+    wide_low = (wide - wide_high.astype(F32)).astype(BF16)
+    restrict[...] = jnp.concatenate([wide_high, wide_low, wide_high], axis=1)
+    prolong[...] = jnp.concatenate(
+        [wide_high.astype(F32), wide_low.astype(F32)], axis=0
+    ).T.astype(BF16)
+
+    def restricted(values):
+        high_part = values.astype(BF16)
+        low_part = (values - high_part.astype(F32)).astype(BF16)
+        return dot(restrict[...], jnp.concatenate([high_part, high_part, low_part], axis=0))
+
+    def prolonged(rounded):
+        return dot(prolong[...], jnp.concatenate([rounded, rounded], axis=0))
+
 
     owns = keeps & (zl < 2)
     group = lax.rem(zl, 2)
-    four = coarse_ref[pl.ds(4 * group, 4)].reshape(4 * Q, Q)
-    row = lax.broadcasted_iota(jnp.int32, (4 * Q, 4 * Q), 0)
-    col = lax.broadcasted_iota(jnp.int32, (4 * Q, 4 * Q), 1)
-    power = jnp.where(row // Q == col // Q, jnp.concatenate([four] * 4, axis=1), 0.0)
-    chain = (row == col).astype(F32)
-    while chain.shape[1] < SLICES * 4 * Q:
-        chain = jnp.concatenate([dot32(power, chain), chain], axis=1)
-        power = dot32(power, power)
-    strip[:, 0 : SLICES * 4 * Q] = chain
-    strip[:, SLICES * 4 * Q :] = jnp.zeros((4 * Q, SLICES * 4 * Q), F32)
-    near = strip[:, pl.ds(pl.multiple_of((3 - x) * 256, 256), 1280)]
-    for d in range(9):
-        first = (8 - d) * 4 * Q
-        part = near[:, first : first + SLICES * 4 * Q]
-        high_part = part.astype(BF16)
-        toep_high[d * 4 * Q : (d + 1) * 4 * Q, :] = high_part
-        toep_low[d * 4 * Q : (d + 1) * 4 * Q, :] = (part - high_part.astype(F32)).astype(BF16)
+    @pl.when(owns)
+    def _():
+        four = coarse_ref[pl.ds(4 * group, 4)].reshape(4 * Q, Q)
+        row = lax.broadcasted_iota(jnp.int32, (4 * Q, 4 * Q), 0)
+        col = lax.broadcasted_iota(jnp.int32, (4 * Q, 4 * Q), 1)
+        power = jnp.where(row // Q == col // Q, jnp.concatenate([four] * 4, axis=1), 0.0)
+        chain = (row == col).astype(F32)
+        while chain.shape[1] < SLICES * 4 * Q:
+            chain = jnp.concatenate([dot32(power, chain), chain], axis=1)
+            power = dot32(power, power)
+        strip[:, 0 : SLICES * 4 * Q] = chain
+        strip[:, SLICES * 4 * Q :] = jnp.zeros((4 * Q, SLICES * 4 * Q), F32)
+        near = strip[:, pl.ds(pl.multiple_of((3 - x) * 256, 256), 1280)]
+        for d in range(9):
+            first = (8 - d) * 4 * Q
+            part = near[:, first : first + SLICES * 4 * Q]
+            high_part = part.astype(BF16)
+            toep_high[d * 4 * Q : (d + 1) * 4 * Q, :] = high_part
+            toep_low[d * 4 * Q : (d + 1) * 4 * Q, :] = (part - high_part.astype(F32)).astype(BF16)
 
     tall = jnp.concatenate([modes] * 16, axis=0).T
     row = lax.broadcasted_iota(jnp.int32, (BRICK, ENS), 0) * 0 + 8 * c
@@ -179,14 +201,15 @@
     @pl.when(moves)
     def _():
         arrived(weights.at[pl.ds(0, 2)], weight_sem)
-        for d in range(1, 4):
+        for d in (1, 3):
             remote(
                 weights.at[fetched], weights.at[fetched], row_send, row_recv,
                 (lax.rem(x + d, 4) * 8 + zl * 2 + c, sp),
             ).start()
         field(0).start()
         field(1).start()
-        arrived(weights.at[pl.ds(0, 6)], row_recv)
+        arrived(weights.at[pl.ds(0, 2)], far_sem)
+        arrived(weights.at[pl.ds(0, 4)], row_recv)
 
     brick_ids = lax.broadcasted_iota(jnp.int32, (HERE, 128), 0)
     shift = lax.rem(nbr[...] - (8 * q + brick_ids) + (REACH + 64), 64)
@@ -227,16 +250,19 @@
             in_plane(lax.rem(q + 7 + 2 * g, HERE)),
         )
 
+    def solved(g, values):
+        return dot(diag[g], values.astype(BF16))
+
     def send_half(u, sweep, g, values):
-        exts[u][sweep][rows_of(g), :] = dot(diag[g], values.astype(BF16)).astype(BF16)
+        exts[u][sweep][rows_of(g), :] = values.astype(BF16)
         halo(u, sweep, g).start()
 
-    def uncoupled(u, sweep, g):
+    def swept(u, sweep, g):
         ext = exts[u][sweep]
         near = dot(band[g, :, : 2 * HALF], ext[0 : 2 * HALF, :])
+        inner = solved(g, (state, columns)[u][rows_of(g), :] - near)
         arrived(ext.at[rows_of(2 + g)], halo_recv.at[u, sweep, g])
-        far = dot(band[g, :, 2 * HALF :], ext[rows_of(2 + g), :])
-        return (state, columns)[u][rows_of(g), :] - near - far
+        return inner - dot(folded[g], ext[rows_of(2 + g), :])
 
     def halves(g):
         return slice(g * HALF, (g + 1) * HALF)
@@ -276,7 +302,9 @@
 
     for u, ref in enumerate((state, columns)):
         for g in (slow, fast):
-            send_half(u, 0, g, ref[rows_of(g), :])
+            send_half(u, 0, g, solved(g, ref[rows_of(g), :]))
+    for g in range(2):
+        folded[g] = dot(diag[g], band[g, :, 2 * HALF :]).astype(BF16)
 
     @pl.loop(0, STEPS)
     def _(i):
@@ -286,11 +314,11 @@
 
         for g in (fast, slow):
             for u in range(2):
-                send_half(u, 1, g, uncoupled(u, 0, g))
+                send_half(u, 1, g, swept(u, 0, g))
         arrived(fields.at[i], field_sem.at[i])
         for g in (fast, slow):
             for u in range(2):
-                following = dot(diag[g], uncoupled(u, 1, g).astype(BF16))
+                following = swept(u, 1, g)
                 arrived(ext00.at[rows_of(0)], halo_send.at[u, 0, g])
                 arrived(ext00.at[rows_of(0)], halo_send.at[u, 1, g])
                 if u == 0:
@@ -303,7 +331,7 @@
 
                 @pl.when(i < STEPS - 1)
                 def _():
-                    send_half(u, 0, g, following)
+                    send_half(u, 0, g, solved(g, following))
 
         @pl.when(i < STEPS - 1)
         def _():
@@ -316,8 +344,6 @@
         @pl.when((i > 0) & keeps)
         def _():
             forward(i - 1)
-
-    prolong = restrict[...].T
 
     def coarse_part(ref, i, gathered, g):
         matrix = jnp.concatenate([ref[i, n, halves(g), :] for n in range(4)], axis=1)
@@ -331,9 +357,9 @@
             defect = state[halves(g), :]
             if it:
                 defect += coarse_part(powers, STEPS - 1, all0, g)
-                defect -= dot32(prolong, sum_here[g])
+                defect -= prolonged(got0[g, 1])
                 stage[STEPS, halves(g), :] = defect.astype(BF16)
-            r_buf[it, g] = dot32(restrict[...], defect).astype(BF16)
+            r_buf[it, g] = restricted(defect).astype(BF16)
 
         @pl.loop(0, 8)
         def _(w):
@@ -445,8 +471,8 @@
         pltpu.make_async_copy(stage.at[i], sol_ref.at[i], sol_recv).start()
     arrived(home_here, here_recv)
     for g in range(2):
-        part = home_here[g * 4 * Q : (g + 1) * 4 * Q, :].astype(F32)
-        stage[STEPS - 1, halves(g), :] = dot32(prolong, part).astype(BF16)
+        part = home_here[g * 4 * Q : (g + 1) * 4 * Q, :]
+        stage[STEPS - 1, halves(g), :] = prolonged(part).astype(BF16)
     pltpu.make_async_copy(stage.at[STEPS - 1], sol_ref.at[STEPS - 1], sol_recv).start()
 
     for it, incoming in enumerate((in0, in1)):
@@ -474,8 +500,8 @@
     def _():
         arrived(all0, all_send.at[1])
         arrived(home_nbr, swap_send.at[5])
-        arrived(weights.at[pl.ds(0, 2)], swap_send.at[4])
-        arrived(weights.at[pl.ds(0, 6)], row_send)
+        arrived(weights.at[pl.ds(0, 2)], swap_send.at[7])
+        arrived(weights.at[pl.ds(0, 4)], row_send)
         for i in range(STEPS):
             arrived(fields.at[i], swap_send.at[i])
         for i in range(STEPS - 1):
@@ -513,8 +539,10 @@
             pltpu.VMEM((ROWS, ENS), F32),
             pltpu.VMEM((2, HALF, 3 * HALF), BF16),
             pltpu.VMEM((2, HALF, HALF), BF16),
+            pltpu.VMEM((2, HALF, HALF), BF16),
             *[pltpu.VMEM((4 * HALF, ENS), BF16)] * 4,
-            pltpu.VMEM((4 * Q, HALF), F32),
+            pltpu.VMEM((4 * Q, 3 * HALF), BF16),
+            pltpu.VMEM((HALF, 8 * Q), BF16),
             pltpu.VMEM((4 * Q, 2 * SLICES * 4 * Q), F32),
             pltpu.VMEM((9 * 4 * Q, SLICES * 4 * Q), BF16),
             pltpu.VMEM((9 * 4 * Q, SLICES * 4 * Q), BF16),
@@ -533,9 +561,10 @@
             sem,
             sem,
             sem,
+            sem,
             sem((2, 2, 2)),
             sem((2, 2, 2)),
-            sem((7,)),
+            sem((8,)),
             sem,
             sem,
             sem((ITERS, 2)),

time: 100 us -> 96.8 us (0.968)
  Pallas kernels: 96.7 us -> 93.1 us
    pallas_call x1, Pallas kernels: 96.7 us -> 93.1 us  [body(): pl.pallas_call(kernel, out_shape=(jax.ShapeDtypeStruct((STEPS, ROWS, ENS)...]
where the time goes in v4:
time: 96.8 us; the launch traced here: 96.6 us
  Pallas kernels  93.1 us (96%)
  other arithmetic  2.88 us (3%)
    pallas_call x1, Pallas kernels, body(): pl.pallas_call(kernel, out_shape=(jax.ShapeDtypeStruct((STEPS, ROWS, ENS)...  93.1 us
    reshape x1, other arithmetic, body(): sol.astype(F32).reshape(STEPS, HERE, BRICK, ENS)  2.16 us

profile of v4, /device:TPU:7, one launch (start us, length us, event | category | flops | bytes accessed | tf_op | source)
XLA Modules:
  0.0 96.6 jit_solution(6754951643597432294)
XLA Ops:
  0.6 93.1 %shard_map.77 = (bf16[4,512,128]{2,1,0:T(8,128)(2,1)}, bf16[512,128]{1,0:T(8,128)(2,1)}) custom-call(f32[512,128]{1,0:T(8,128)} %bitcast.8, bf16[4,512,128]{2,1,0:T(8,128)(2,1)} %bitcast.7, bf16[8,64,448]{2,1,0:T(8,128)(2,1)} %blocks_ref.1, s32[8,6]{1,0:T(8,128)} %neighbours_ref.1, f32[8,64]{1,0:T(8,128)} %modes_ref.1, f32[8,8,8]{2,1,0:T(8,128)} %coarse_ref.1), custom_call_target="tpu_custom_call" | custom-call | tf_op jit(solution)/shard_map/pallas_call | solution.py:524
  93.7 0.0 copy-start
  93.7 2.2 %convert.2 = f32[4,8,64,128]{3,2,1,0:T(8,128)} convert(bf16[4,8,64,128]{3,2,1,0:T(8,128)(2,1)} %bitcast.6) | non-fusion elementwise | flops 262144 | bytes 1572864 | tf_op jit(solution)/shard_map/reshape | solution.py:598
  95.9 0.0 copy-done
  95.9 0.7 convert.3
Async XLA Ops:
  93.7 2.2 %copy-start = (bf16[512,128]{1,0:T(8,128)(2,1)S(1)}, bf16[512,128]{1,0:T(8,128)(2,1)}, u32[]{:S(2)}) copy-start(bf16[512,128]{1,0:T(8,128)(2,1)} %get-tuple-element.5) | copy-start | bytes 393220

commit v5 on v4

--- a/solution.py
+++ b/solution.py
@@ -37,7 +37,7 @@
     init_ref, forcing_ref, blocks_ref, neighbours_ref, modes_ref, coarse_ref,
     sol_ref, def_ref,
     fields, weights, home_nbr, nbr, start, state, columns, band, folded, diag, ext00, ext01, ext10, ext11,
-    restrict, prolong, strip, toep_high, toep_low, r_buf, in0, in1, err0, err1, got0, got1, all0, all1,
+    restrict, prolong, coarse_map, strip, toep_high, toep_low, r_buf, in0, in1, err0, err1, got0, got1, all0, all1,
     powers, home_powers, held, home_held, prev_buf, here_buf, home_here, stage,
     field_sem, weight_sem, far_sem, nbr_sem, start_sem, halo_send, halo_recv, swap_send, row_send, row_recv,
     sc_send, sc_recv, all_send, all_recv, power_send, power_recv, forward_send, home_power_sem,
@@ -300,67 +300,7 @@
     def _():
         state[...] = jnp.zeros_like(state)
 
-    for u, ref in enumerate((state, columns)):
-        for g in (slow, fast):
-            send_half(u, 0, g, solved(g, ref[rows_of(g), :]))
-    for g in range(2):
-        folded[g] = dot(diag[g], band[g, :, 2 * HALF :]).astype(BF16)
-
-    @pl.loop(0, STEPS)
-    def _(i):
-        @pl.when(moves & (i < 2))
-        def _():
-            field(i + 2).start()
-
-        for g in (fast, slow):
-            for u in range(2):
-                send_half(u, 1, g, swept(u, 0, g))
-        arrived(fields.at[i], field_sem.at[i])
-        for g in (fast, slow):
-            for u in range(2):
-                following = swept(u, 1, g)
-                arrived(ext00.at[rows_of(0)], halo_send.at[u, 0, g])
-                arrived(ext00.at[rows_of(0)], halo_send.at[u, 1, g])
-                if u == 0:
-                    following += fields[i, rows_of(g), :].astype(F32)
-                    state[rows_of(g), :] = following
-                    held[i, rows_of(g), :] = following.astype(BF16)
-                else:
-                    columns[rows_of(g), :] = following
-                    powers[i, x, rows_of(g), :] = following.astype(BF16)
-
-                @pl.when(i < STEPS - 1)
-                def _():
-                    send_half(u, 0, g, solved(g, following))
-
-        @pl.when(i < STEPS - 1)
-        def _():
-            bring(held.at[i], home_held.at[i], held_send.at[i], home_held_sem.at[i])
-
-        @pl.when((i < STEPS - 1) & keeps)
-        def _():
-            share(i)
-
-        @pl.when((i > 0) & keeps)
-        def _():
-            forward(i - 1)
-
-    def coarse_part(ref, i, gathered, g):
-        matrix = jnp.concatenate([ref[i, n, halves(g), :] for n in range(4)], axis=1)
-        return dot(matrix, gathered[...])
-
-    sum_prev = sum_here = None
-    for it, (incoming, err, got, gathered) in enumerate(
-        ((in0, err0, got0, all0), (in1, err1, got1, all1))
-    ):
-        for g in range(2):
-            defect = state[halves(g), :]
-            if it:
-                defect += coarse_part(powers, STEPS - 1, all0, g)
-                defect -= prolonged(got0[g, 1])
-                stage[STEPS, halves(g), :] = defect.astype(BF16)
-            r_buf[it, g] = restricted(defect).astype(BF16)
-
+    def to_owners(it, incoming):
         @pl.loop(0, 8)
         def _(w):
             g = lax.rem(w, 2)
@@ -378,6 +318,73 @@
                     r_buf.at[it, g], incoming.at[j], sc_send.at[it, 0], sc_recv.at[it, 0],
                     (owner_tm, owner_sp),
                 ).start()
+
+    for u, ref in enumerate((state, columns)):
+        for g in (slow, fast):
+            send_half(u, 0, g, solved(g, ref[rows_of(g), :]))
+    for g in range(2):
+        folded[g] = dot(diag[g], band[g, :, 2 * HALF :]).astype(BF16)
+
+    @pl.loop(0, STEPS)
+    def _(i):
+        @pl.when(moves & (i < 2))
+        def _():
+            field(i + 2).start()
+
+        for g in (fast, slow):
+            for u in range(2):
+                send_half(u, 1, g, swept(u, 0, g))
+        arrived(fields.at[i], field_sem.at[i])
+        for g, u in ((fast, 0), (fast, 1), (slow, 0), (slow, 1)):
+            following = swept(u, 1, g)
+            arrived(ext00.at[rows_of(0)], halo_send.at[u, 0, g])
+            arrived(ext00.at[rows_of(0)], halo_send.at[u, 1, g])
+            if u == 0:
+                following += fields[i, rows_of(g), :].astype(F32)
+                state[rows_of(g), :] = following
+
+                @pl.when(i == STEPS - 1)
+                def _():
+                    r_buf[0, g] = restricted(following).astype(BF16)
+                    if g is slow:
+                        to_owners(0, in0)
+
+                held[i, rows_of(g), :] = following.astype(BF16)
+            else:
+                columns[rows_of(g), :] = following
+                powers[i, x, rows_of(g), :] = following.astype(BF16)
+
+            @pl.when(i < STEPS - 1)
+            def _():
+                send_half(u, 0, g, solved(g, following))
+
+        @pl.when(i < STEPS - 1)
+        def _():
+            bring(held.at[i], home_held.at[i], held_send.at[i], home_held_sem.at[i])
+
+        @pl.when((i < STEPS - 1) & keeps)
+        def _():
+            share(i)
+
+        @pl.when((i > 0) & keeps)
+        def _():
+            forward(i - 1)
+
+    def coarse_part(ref, i, gathered, g):
+        matrix = jnp.concatenate([ref[i, n, halves(g), :] for n in range(4)], axis=1)
+        return dot(matrix, gathered[...])
+
+    sum_prev = sum_here = None
+    for it, (incoming, err, got, gathered) in enumerate(
+        ((in0, err0, got0, all0), (in1, err1, got1, all1))
+    ):
+        if it:
+            for g in range(2):
+                r_buf[1, g] = (known[g] + dot(coarse_map[g], all0[...])).astype(BF16)
+            to_owners(1, in1)
+            for g in range(2):
+                defect = state[halves(g), :] + coarse_part(powers, STEPS - 1, all0, g)
+                stage[STEPS, halves(g), :] = (defect - prolonged(got0[g, 1])).astype(BF16)
 
         if it:
             bring(stage.at[STEPS], def_ref, out_send, def_recv)
@@ -430,7 +437,13 @@
                     in_plane(lax.rem(q + d, HERE)),
                 ).start()
 
+            known = [restricted(state[halves(g), :] - prolonged(got[g, 1])) for g in range(2)]
             arrived(powers.at[STEPS - 1, pl.ds(0, 3)], power_recv.at[STEPS - 1])
+            for g in range(2):
+                last = [powers[STEPS - 1, n, halves(g), :] for n in range(4)]
+                last = jnp.concatenate(last, axis=1)
+                last = jnp.concatenate([last, last], axis=0)
+                coarse_map[g] = dot(restrict[:, : 2 * HALF], last).astype(BF16)
             arrived(gathered.at[pl.ds(0, 7 * HERE * Q)], all_recv.at[it])
         else:
             prev_buf[...] = rounded_prev
@@ -543,6 +556,7 @@
             *[pltpu.VMEM((4 * HALF, ENS), BF16)] * 4,
             pltpu.VMEM((4 * Q, 3 * HALF), BF16),
             pltpu.VMEM((HALF, 8 * Q), BF16),
+            pltpu.VMEM((2, 4 * Q, HERE * HERE * Q), BF16),
             pltpu.VMEM((4 * Q, 2 * SLICES * 4 * Q), F32),
             pltpu.VMEM((9 * 4 * Q, SLICES * 4 * Q), BF16),
             pltpu.VMEM((9 * 4 * Q, SLICES * 4 * Q), BF16),

time: 96.8 us -> 94.6 us (0.977)
  the two profiles are of different devices: /device:TPU:7 before, /device:TPU:1 now
where the time goes in v5:
time: 94.6 us; the launch traced here: 94.5 us
  Pallas kernels  90.9 us (96%)
  other arithmetic  2.88 us (3%)
    pallas_call x1, Pallas kernels, body(): pl.pallas_call(kernel, out_shape=(jax.ShapeDtypeStruct((STEPS, ROWS, ENS)...  90.9 us
    reshape x1, other arithmetic, body(): sol.astype(F32).reshape(STEPS, HERE, BRICK, ENS)  2.16 us

profile of v5, /device:TPU:1, one launch (start us, length us, event | category | flops | bytes accessed | tf_op | source)
XLA Modules:
  0.0 94.5 jit_solution(16258620961666924110)
XLA Ops:
  0.6 90.9 %shard_map.77 = (bf16[4,512,128]{2,1,0:T(8,128)(2,1)}, bf16[512,128]{1,0:T(8,128)(2,1)}) custom-call(f32[512,128]{1,0:T(8,128)} %bitcast.8, bf16[4,512,128]{2,1,0:T(8,128)(2,1)} %bitcast.7, bf16[8,64,448]{2,1,0:T(8,128)(2,1)} %blocks_ref.1, s32[8,6]{1,0:T(8,128)} %neighbours_ref.1, f32[8,64]{1,0:T(8,128)} %modes_ref.1, f32[8,8,8]{2,1,0:T(8,128)} %coarse_ref.1), custom_call_target="tpu_custom_call" | custom-call | tf_op jit(solution)/shard_map/pallas_call | solution.py:537
  91.6 0.0 copy-start
  91.6 2.2 %convert.2 = f32[4,8,64,128]{3,2,1,0:T(8,128)} convert(bf16[4,8,64,128]{3,2,1,0:T(8,128)(2,1)} %bitcast.6) | non-fusion elementwise | flops 262144 | bytes 1572864 | tf_op jit(solution)/shard_map/reshape | solution.py:612
  93.7 0.0 copy-done
  93.7 0.7 convert.3
Async XLA Ops:
  91.6 2.2 %copy-start = (bf16[512,128]{1,0:T(8,128)(2,1)S(1)}, bf16[512,128]{1,0:T(8,128)(2,1)}, u32[]{:S(2)}) copy-start(bf16[512,128]{1,0:T(8,128)(2,1)} %get-tuple-element.5) | copy-start | bytes 393220

commit v6 on v5

--- a/solution.py
+++ b/solution.py
@@ -72,6 +72,8 @@
         for i in range(STEPS):
             pltpu.make_async_copy(forcing_ref.at[i], fields.at[i], field_sem.at[i]).start()
 
+    in0[...] = jnp.zeros_like(in0)
+    in1[...] = jnp.zeros_like(in1)
     barrier = pltpu.get_barrier_semaphore()
 
     @pl.when(moves)
@@ -301,7 +303,7 @@
         state[...] = jnp.zeros_like(state)
 
     def to_owners(it, incoming):
-        @pl.loop(0, 8)
+        @pl.loop(2 * x, 8)
         def _(w):
             g = lax.rem(w, 2)
             owner_tm = (w // 2) * 8 + g * 2 + c
@@ -393,7 +395,12 @@
 
         @pl.when(owns)
         def _():
-            arrived(incoming.at[pl.ds(0, SLICES - 1)], sc_recv.at[it, 0])
+            for quarter in range(4):
+
+                @pl.when(x == quarter)
+                def _():
+                    arrived(incoming.at[pl.ds(0, 8 * quarter + 7)], sc_recv.at[it, 0])
+
             terms = incoming[...].reshape(SLICES * 4 * Q, ENS)
             errors = dot(toep_high[...], terms) + dot(toep_low[...], terms)
             err[...] = errors.astype(BF16).reshape(9, 4 * Q, ENS)
@@ -449,6 +456,8 @@
             prev_buf[...] = rounded_prev
             here_buf[...] = jnp.concatenate(sum_here, axis=0).astype(BF16)
 
+            bring(here_buf, home_here, here_send, here_recv)
+
             @pl.loop(0, HERE)
             def _(d):
                 home = lax.rem(sp + d, HERE)
@@ -465,39 +474,45 @@
                         (tm - c + zh, home),
                     ).start()
 
-            bring(here_buf, home_here, here_send, here_recv)
-
-    @pl.when(keeps)
-    def _():
-        arrived(all1.at[pl.ds(0, 7 * HERE * Q)], all_recv.at[1])
-
-    @pl.when(moves)
-    def _():
-        arrived(all1, all_recv.at[1])
 
     for i in range(STEPS - 1):
         arrived(home_held.at[i], home_held_sem.at[i])
         arrived(home_powers.at[i], home_power_sem.at[i])
-        for g in range(2):
-            value = home_held[i, halves(g), :].astype(F32) + coarse_part(home_powers, i, all1, g)
-            stage[i, halves(g), :] = value.astype(BF16)
-        pltpu.make_async_copy(stage.at[i], sol_ref.at[i], sol_recv).start()
     arrived(home_here, here_recv)
     for g in range(2):
         part = home_here[g * 4 * Q : (g + 1) * 4 * Q, :]
         stage[STEPS - 1, halves(g), :] = prolonged(part).astype(BF16)
     pltpu.make_async_copy(stage.at[STEPS - 1], sol_ref.at[STEPS - 1], sol_recv).start()
 
+    @pl.when(keeps)
+    def _():
+        arrived(all1.at[pl.ds(0, 7 * HERE * Q)], all_recv.at[1])
+
+    @pl.when(moves)
+    def _():
+        arrived(all1, all_recv.at[1])
+
+    for i in range(STEPS - 1):
+        for g in range(2):
+            value = home_held[i, halves(g), :].astype(F32) + coarse_part(home_powers, i, all1, g)
+            stage[i, halves(g), :] = value.astype(BF16)
+        pltpu.make_async_copy(stage.at[i], sol_ref.at[i], sol_recv).start()
+
     for it, incoming in enumerate((in0, in1)):
 
         @pl.when(owns)
         def _():
-            arrived(incoming.at[pl.ds(0, 7)], sc_send.at[it, 0])
             arrived(incoming.at[pl.ds(0, 14)], sc_send.at[it, 1])
 
-        @pl.when(jnp.logical_not(owns))
-        def _():
-            arrived(incoming.at[pl.ds(0, 8)], sc_send.at[it, 0])
+        for quarter in range(4):
+
+            @pl.when(owns & (x == quarter))
+            def _():
+                arrived(incoming.at[pl.ds(0, 7 - 2 * quarter)], sc_send.at[it, 0])
+
+            @pl.when(jnp.logical_not(owns) & (x == quarter))
+            def _():
+                arrived(incoming.at[pl.ds(0, 8 - 2 * quarter)], sc_send.at[it, 0])
 
     arrived(all0.at[pl.ds(0, 7 * HERE * Q)], all_send.at[0])
     arrived(powers.at[STEPS - 1, pl.ds(0, 3)], power_send.at[STEPS - 1])

time: 94.6 us -> 92.4 us (0.977)
  the two profiles are of different devices: /device:TPU:1 before, /device:TPU:7 now
where the time goes in v6:
time: 92.4 us; the launch traced here: 91.9 us
  Pallas kernels  88.4 us (96%)
  other arithmetic  2.88 us (3%)
    pallas_call x1, Pallas kernels, body(): pl.pallas_call(kernel, out_shape=(jax.ShapeDtypeStruct((STEPS, ROWS, ENS)...  88.4 us
    reshape x1, other arithmetic, body(): sol.astype(F32).reshape(STEPS, HERE, BRICK, ENS)  2.16 us

profile of v6, /device:TPU:7, one launch (start us, length us, event | category | flops | bytes accessed | tf_op | source)
XLA Modules:
  0.0 91.9 jit_solution(12181799804947551165)
XLA Ops:
  0.6 88.4 %shard_map.77 = (bf16[4,512,128]{2,1,0:T(8,128)(2,1)}, bf16[512,128]{1,0:T(8,128)(2,1)}) custom-call(f32[512,128]{1,0:T(8,128)} %bitcast.8, bf16[4,512,128]{2,1,0:T(8,128)(2,1)} %bitcast.7, bf16[8,64,448]{2,1,0:T(8,128)(2,1)} %blocks_ref.1, s32[8,6]{1,0:T(8,128)} %neighbours_ref.1, f32[8,64]{1,0:T(8,128)} %modes_ref.1, f32[8,8,8]{2,1,0:T(8,128)} %coarse_ref.1), custom_call_target="tpu_custom_call" | custom-call | tf_op jit(solution)/shard_map/pallas_call | solution.py:552
  89.0 0.0 copy-start
  89.1 2.2 %convert.2 = f32[4,8,64,128]{3,2,1,0:T(8,128)} convert(bf16[4,8,64,128]{3,2,1,0:T(8,128)(2,1)} %bitcast.6) | non-fusion elementwise | flops 262144 | bytes 1572864 | tf_op jit(solution)/shard_map/reshape | solution.py:627
  91.2 0.0 copy-done
  91.2 0.7 convert.3
Async XLA Ops:
  89.0 2.2 %copy-start = (bf16[512,128]{1,0:T(8,128)(2,1)S(1)}, bf16[512,128]{1,0:T(8,128)(2,1)}, u32[]{:S(2)}) copy-start(bf16[512,128]{1,0:T(8,128)(2,1)} %get-tuple-element.5) | copy-start | bytes 393220

commit v7 on v6

--- a/solution.py
+++ b/solution.py
@@ -405,7 +405,7 @@
             errors = dot(toep_high[...], terms) + dot(toep_low[...], terms)
             err[...] = errors.astype(BF16).reshape(9, 4 * Q, ENS)
 
-            @pl.loop(0, 8)
+            @pl.loop(0, 8, unroll=True)
             def _(d):
                 there = x * 8 + d
 
@@ -437,7 +437,7 @@
         if it == 0:
             gathered[mine, :] = rounded_prev
 
-            @pl.loop(1, HERE)
+            @pl.loop(1, HERE, unroll=True)
             def _(d):
                 remote(
                     gathered.at[mine], gathered.at[mine], all_send.at[it], all_recv.at[it],
@@ -458,7 +458,7 @@
 
             bring(here_buf, home_here, here_send, here_recv)
 
-            @pl.loop(0, HERE)
+            @pl.loop(0, HERE, unroll=True)
             def _(d):
                 home = lax.rem(sp + d, HERE)
                 own = keeps & (home == sp)

time: 92.4 us -> 92.4 us (level)
  no operation moved by 1% of the time
where the time goes in v7:
time: 92.4 us; the launch traced here: 91.9 us
  Pallas kernels  88.4 us (96%)
  other arithmetic  2.88 us (3%)
    pallas_call x1, Pallas kernels, body(): pl.pallas_call(kernel, out_shape=(jax.ShapeDtypeStruct((STEPS, ROWS, ENS)...  88.4 us
    reshape x1, other arithmetic, body(): sol.astype(F32).reshape(STEPS, HERE, BRICK, ENS)  2.16 us

profile of v7, /device:TPU:7, one launch (start us, length us, event | category | flops | bytes accessed | tf_op | source)
XLA Modules:
  0.0 91.9 jit_solution(8453131036940528503)
XLA Ops:
  0.6 88.4 %shard_map.77 = (bf16[4,512,128]{2,1,0:T(8,128)(2,1)}, bf16[512,128]{1,0:T(8,128)(2,1)}) custom-call(f32[512,128]{1,0:T(8,128)} %bitcast.8, bf16[4,512,128]{2,1,0:T(8,128)(2,1)} %bitcast.7, bf16[8,64,448]{2,1,0:T(8,128)(2,1)} %blocks_ref.1, s32[8,6]{1,0:T(8,128)} %neighbours_ref.1, f32[8,64]{1,0:T(8,128)} %modes_ref.1, f32[8,8,8]{2,1,0:T(8,128)} %coarse_ref.1), custom_call_target="tpu_custom_call" | custom-call | tf_op jit(solution)/shard_map/pallas_call | solution.py:552
  89.0 0.0 copy-start
  89.0 2.2 %convert.2 = f32[4,8,64,128]{3,2,1,0:T(8,128)} convert(bf16[4,8,64,128]{3,2,1,0:T(8,128)(2,1)} %bitcast.6) | non-fusion elementwise | flops 262144 | bytes 1572864 | tf_op jit(solution)/shard_map/reshape | solution.py:627
  91.2 0.0 copy-done
  91.2 0.7 convert.3
Async XLA Ops:
  89.0 2.2 %copy-start = (bf16[512,128]{1,0:T(8,128)(2,1)S(1)}, bf16[512,128]{1,0:T(8,128)(2,1)}, u32[]{:S(2)}) copy-start(bf16[512,128]{1,0:T(8,128)(2,1)} %get-tuple-element.5) | copy-start | bytes 393220
